TPU v7x, 32 devices: a whole 2x2x4 slice. The times are simulated.
32 devices in a mesh: group: 2 (over y), pool: 8 (over z, x), tp: 2 (over core).
Axes of the slice: x: 2, y: 2, z: 4, core: 2. Of those that a mesh axis runs over, the one named last changes fastest.
Arguments:
- queries: bfloat16 [64, 16384], P(('group', 'pool'), 'tp'), parts along dimension 0, may hold values from -16 to 16
- keys: bfloat16 [64, 1024, 256], P(('group', 'pool')), parts along dimension 0, may hold values from -6 to 6
- values: bfloat16 [64, 1024, 256], P(('group', 'pool')), parts along dimension 0, may hold values from -6 to 6
- lengths: int32 [64], P(('group', 'pool')), parts along dimension 0, may hold values from 128 to 1024, as said below
- moe_input: bfloat16 [256, 7168], P(('group', 'pool')), parts along dimension 0, may hold values from -6 to 6
- routes: int32 [256, 3], P(('group', 'pool')), parts along dimension 0, may hold values from 0 to 7, all different within a row; in each aligned block of 16 rows (0 to 15, 16 to 31, ...) at most 8 rows name the same one
- gate_level: int32 [256, 3], P(('group', 'pool')), parts along dimension 0, may hold values from 64 to 1024
- w_gate: bfloat16 [8, 7168, 2560], P('pool', None, 'tp'), may hold values from -0.0625 to 0.0625
- w_up: bfloat16 [8, 7168, 2560], P('pool', None, 'tp'), may hold values from -0.0625 to 0.0625
- w_down: bfloat16 [8, 2560, 7168], P('pool', 'tp'), may hold values from -0.125 to 0.125
Outputs:
- context: bfloat16 [64, 16384], P(('group', 'pool'), 'tp'), parts along dimension 0
- moe_output: bfloat16 [256, 7168], P(('group', 'pool'), 'tp'), parts along dimension 0
There are 2 independent parts, one for each index of `group`. A program takes and returns all parts, laid end to end along the dimension named above; an argument that names none is the same for every part. Nothing has to cross between parts.
Inputs may be any that keep to these rules, and one draw needn't show every extreme that they name: `lengths`: some request has all 1024 slots live in every draw. `routes`: the rows of one index of pool name no expert more than 8 times; some expert exactly 8 times.
All inputs are finite; a program needn't handle non-finite values.
Results may differ from a plain program's by a relative error of at most 0.005.
Values may be sent and summed in bfloat16 or wider, within the bound.
No kernel may reach another device: no remote copies, remote signals or barrier semaphores. Data moves between devices by JAX's collectives and lax.ppermute only.
A program may use at most 128 MiB of HBM per device.

v0:
```python
import jax
import jax.numpy as jnp
from jax import lax
from jax.sharding import PartitionSpec as P

HDIM = 256
EXPERTS = 8
TOP = 3


def attention(queries, keys, values, lengths):
    requests_here = queries.shape[0]
    heads_here = queries.shape[1] // HDIM
    query_heads = queries.reshape(requests_here, heads_here, HDIM)
    scores = jnp.einsum(
        "rhd,rkd->rhk", query_heads, keys, preferred_element_type=jnp.float32
    ) * HDIM ** (-0.5)
    live = jnp.arange(keys.shape[1], dtype=jnp.int32)[None, :] < lengths[:, None]
    scores = jnp.where(live[:, None, :], scores, -1e30)
    top = jnp.max(scores, axis=2, keepdims=True)
    weights = jnp.exp(scores - top)
    total = jnp.sum(weights, axis=2, keepdims=True)
    summed = jnp.einsum(
        "rhk,rkd->rhd", weights.astype(jnp.bfloat16), values, preferred_element_type=jnp.float32
    )
    return (summed / total).astype(jnp.bfloat16).reshape(requests_here, heads_here * HDIM)


def body(queries, keys, values, lengths, moe_input, routes, gate_level, w_gate, w_up, w_down):
    context = attention(queries, keys, values, lengths)
    rows_here = moe_input.shape[0]
    width = moe_input.shape[1]
    capacity = rows_here // 2
    pool_count = lax.axis_size("pool")
    span = pool_count // EXPERTS
    flat_routes = routes.reshape(-1)
    onehot = (flat_routes[:, None] == jnp.arange(EXPERTS, dtype=jnp.int32)[None, :]).astype(
        jnp.int32
    )
    earlier = jnp.cumsum(onehot, axis=0) - onehot
    rank = jnp.sum(onehot * earlier, axis=1)
    position = flat_routes * capacity + rank
    match = position[:, None] == jnp.arange(EXPERTS * capacity, dtype=jnp.int32)[None, :]
    placing = jnp.sum(match.reshape(rows_here, TOP, EXPERTS * capacity), axis=1).T.astype(
        jnp.bfloat16
    )
    gate_weight = gate_level.reshape(-1).astype(jnp.float32) / 1024.0
    combining = jnp.sum(
        (match.astype(jnp.float32) * gate_weight[:, None]).reshape(
            rows_here, TOP, EXPERTS * capacity
        ),
        axis=1,
    )
    slots = jnp.dot(placing, moe_input, preferred_element_type=jnp.float32).astype(jnp.bfloat16)
    slots = slots.reshape(EXPERTS, 1, capacity, width)
    outgoing = jnp.broadcast_to(slots, (EXPERTS, span, capacity, width)).reshape(
        pool_count, capacity, width
    )
    received = lax.all_to_all(outgoing, "pool", split_axis=0, concat_axis=0, tiled=True)
    flat_rows = received.reshape(pool_count * capacity, width)
    gate = jnp.dot(flat_rows, w_gate[0], preferred_element_type=jnp.float32)
    upper = jnp.dot(flat_rows, w_up[0], preferred_element_type=jnp.float32)
    hidden = (jax.nn.silu(gate) * upper).astype(jnp.bfloat16)
    partial_value = jnp.dot(hidden, w_down[0], preferred_element_type=jnp.float32).reshape(
        pool_count, capacity, width
    )
    returned = lax.all_to_all(partial_value, "pool", split_axis=0, concat_axis=0, tiled=True)
    gathered = jnp.sum(returned.reshape(EXPERTS, span, capacity, width), axis=1).reshape(
        EXPERTS * capacity, width
    )
    mixed = jnp.dot(
        combining, gathered, precision=lax.Precision.HIGHEST, preferred_element_type=jnp.float32
    )
    moe_output = lax.psum_scatter(mixed, "tp", scatter_dimension=1, tiled=True).astype(jnp.bfloat16)
    return (context, moe_output)


def solution(mesh):
    return jax.shard_map(
        body,
        mesh=mesh,
        in_specs=(
            P(("group", "pool"), "tp"),
            P(("group", "pool"), None, None),
            P(("group", "pool"), None, None),
            P(("group", "pool")),
            P(("group", "pool"), None),
            P(("group", "pool"), None),
            P(("group", "pool"), None),
            P("pool", None, "tp"),
            P("pool", None, "tp"),
            P("pool", "tp", None),
        ),
        out_specs=(P(("group", "pool"), "tp"), P(("group", "pool"), "tp")),
        check_vma=False,
    )
```

profile of v0, /device:TPU:0, one launch (start us, length us, event | category | flops | bytes accessed | tf_op | source)
XLA Modules:
  0.0 134.5 jit_solution(17378961205762127807)
XLA Ops:
  7.2 0.0 copy-start
  7.2 0.9 copy.21
  8.1 0.1 eq.30
  8.2 0.1 fusion.39
  8.2 0.1 reduce_window_sum.11
  8.3 0.2 select_reduce_fusion.1
  8.5 0.1 reduce_sum.44
  8.6 0.1 copy.22
  8.7 0.7 multiply_add_fusion
  9.4 0.1 convert_reduce_fusion
  9.5 1.4 %fusion.6 = bf16[8,8,7168]{2,1,0:T(8,128)(2,1)S(1)} fusion(bf16[16,7168]{1,0:T(8,128)(2,1)} %param.14, s32[16,64]{1,0:T(8,128)S(1)} %convert_reduce_fusion), kind=kOutput, calls=%fused_computation.7 | convolution fusion | flops 15139840 | bytes 1150976 | tf_op jit(solution)/shard_map/dot_general | solution.py:54
  10.8 30.4 %all_to_all.10 = bf16[8,8,7168]{2,1,0:T(8,128)(2,1)S(1)} all-to-all(bf16[8,8,7168]{2,1,0:T(8,128)(2,1)S(1)} %fusion.6), channel_id=1, replica_groups=mesh['group'=2,'pool'=8,'tp'=2] {'pool'}, dimensions={0} | all-to-all | bytes 1835008 | tf_op jit(solution)/shard_map/all_to_all | solution.py:59
  41.2 9.5 %fusion.4 = f32[64,1280]{1,0:T(8,128)S(1)} fusion(bf16[1,7168,1280]{2,1,0:T(8,128)(2,1)} %param.17, bf16[8,8,7168]{2,1,0:T(8,128)(2,1)S(1)} %all_to_all.10), kind=kOutput, calls=%fused_computation.4 | convolution fusion | flops 1174405120 | bytes 19595264 | tf_op jit(solution)/shard_map/dot_general | solution.py:61
  50.7 19.1 %fusion = f32[8,8,7168]{2,1,0:T(8,128)} fusion(bf16[1,1280,7168]{2,1,0:T(8,128)(2,1)} %param.19, bf16[1,7168,1280]{2,1,0:T(8,128)(2,1)} %param.18, bf16[8,8,7168]{2,1,0:T(8,128)(2,1)S(1)} %all_to_all.10, f32[64,1280]{1,0:T(8,128)S(1)} %fusion.4), kind=kOutput, calls=%fused_computation | convolution fusion | flops 2349301760 | bytes 39780352 | tf_op jit(solution)/shard_map/dot_general | solution.py:64
  69.8 4.4 %all-to-all-start.1 = ((f32[8,8,7168]{2,1,0:T(8,128)}), f32[8,8,7168]{2,1,0:T(8,128)}, u32[]{:S(2)}, u32[]{:S(2)}) async-start(f32[8,8,7168]{2,1,0:T(8,128)} %fusion), calls=%async_computation.1 | async-start | bytes 3670016 | tf_op jit(solution)/shard_map/all_to_all | solution.py:67
  74.2 0.0 copy-start.4
  74.2 0.0 copy-start.2
  74.2 0.0 reduce-scatter.2.cloned.1.call-start
  74.3 0.0 copy-done.3
  74.3 0.1 select_reduce_fusion
  74.4 41.3 %all-to-all-done.1 = f32[8,8,7168]{2,1,0:T(8,128)} async-done(((f32[8,8,7168]{2,1,0:T(8,128)}), f32[8,8,7168]{2,1,0:T(8,128)}, u32[]{:S(2)}, u32[]{:S(2)}) %all-to-all-start.1) | async-done | bytes 1835040 | tf_op jit(solution)/shard_map/all_to_all | solution.py:67
  115.7 3.3 %fusion.16 = f32[16,7168]{1,0:T(8,128)} fusion(f32[16,64]{1,0:T(8,128)S(1)} %select_reduce_fusion, f32[8,8,7168]{2,1,0:T(8,128)} %all-to-all-done.1), kind=kOutput, calls=%fused_computation.11 | convolution fusion | flops 88080384 | bytes 2297856 | tf_op jit(solution)/shard_map/dot_general | solution.py:71
  119.0 0.0 reduce-scatter.2.cloned.1.call-update
  119.0 0.0 copy-start.1
  119.0 0.1 iota_compare_fusion.2
  119.1 0.8 fusion.42
  119.9 0.2 fusion.27
  120.2 0.5 copy-done.1
  120.6 0.5 fusion.20
  121.1 0.7 copy.24
  121.8 4.2 %reduce-scatter.2.cloned.1.call-done = f32[16,3584]{1,0:T(8,128)} async-done(((f32[16,7168]{1,0:T(8,128)}), f32[16,3584]{1,0:T(8,128)}) %reduce-scatter.2.cloned.1.call-update) | async-done | bytes 229392 | tf_op jit(solution)/shard_map/reduce_scatter | solution.py:74
  126.0 1.6 %convert_element_type.41 = bf16[16,3584]{1,0:T(8,128)(2,1)} convert(f32[16,3584]{1,0:T(8,128)} %reduce-scatter.2.cloned.1.call-done) | non-fusion elementwise | flops 57344 | bytes 344064 | tf_op jit(solution)/shard_map/convert_element_type | solution.py:74
  (5 shorter events, 0.0 us)
Async XLA Ops:
  7.2 111.9 %copy-start = (bf16[4,1024,256]{2,1,0:T(8,128)(2,1)S(1)}, bf16[4,1024,256]{2,1,0:T(8,128)(2,1)}, u32[]{:S(2)}) copy-start(bf16[4,1024,256]{2,1,0:T(8,128)(2,1)} %param.11) | copy-start | bytes 6291460
  69.8 4.5 %copy-start.3 = (s32[16,3]{0,1:T(4,128)S(1)}, s32[16,3]{0,1:T(4,128)}, u32[]{:S(2)}) copy-start(s32[16,3]{0,1:T(4,128)} %param.16) | copy-start | bytes 580
  69.8 46.0 %all-to-all-start.1 = ((f32[8,8,7168]{2,1,0:T(8,128)}), f32[8,8,7168]{2,1,0:T(8,128)}, u32[]{:S(2)}, u32[]{:S(2)}) async-start(f32[8,8,7168]{2,1,0:T(8,128)} %fusion), calls=%async_computation.1 | async-start | bytes 3670016 | tf_op jit(solution)/shard_map/all_to_all | solution.py:67
  74.2 44.8 %copy-start.4 = (s32[4]{0:T(128)S(1)}, s32[4]{0:T(128)}, u32[]{:S(2)}) copy-start(s32[4]{0:T(128)} %param.13) | copy-start | bytes 52
  74.2 44.9 %copy-start.2 = (bf16[4,8192]{1,0:T(4,128)(2,1)S(1)}, bf16[4,8192]{1,0:T(4,128)(2,1)}, u32[]{:S(2)}) copy-start(bf16[4,8192]{1,0:T(4,128)(2,1)} %param.10) | copy-start | bytes 196612
  74.2 51.8 %reduce-scatter.2.cloned.1.call-start = ((), (), s32[]{:S(2)}) async-start(), calls=%async_computation.3 | async-start | bytes 688128 | tf_op jit(solution)/shard_map/reduce_scatter | solution.py:74
  119.0 1.6 %copy-start.1 = (bf16[4,1024,256]{2,1,0:T(8,128)(2,1)S(1)}, bf16[4,1024,256]{2,1,0:T(8,128)(2,1)}, u32[]{:S(2)}) copy-start(bf16[4,1024,256]{2,1,0:T(8,128)(2,1)} %param.12) | copy-start | bytes 6291460
Sparse Core Ops, SparseCore 0:
  119.1 6.8 reduce-scatter.1
where the time goes:
time: 135 us; the launch traced here: 134 us
  waiting for transfers between devices  45.6 us (34%)
  matrix products  34.5 us (26%)
  blocking collectives  30.4 us (23%)
  between operations  14.1 us (10%)
  starting transfers between devices  4.48 us (3%)
  other arithmetic  3.09 us (2%)
  local copies, waits for them, and re-layouts  2.34 us (2%)
    all_to_all x1, waiting for transfers between devices, body(): lax.all_to_all(partial_value, 'pool', split_axis=0, concat_axis=0, tiled=...  41.3 us
    all_to_all x1, blocking collectives, body(): lax.all_to_all(outgoing, 'pool', split_axis=0, concat_axis=0, tiled=True)  30.4 us
    dot_general x1, matrix products, body(): jnp.dot(hidden, w_down[0], preferred_element_type=jnp.float32)  19.1 us
    dot_general x1, matrix products, body(): gate = jnp.dot(flat_rows, w_gate[0], preferred_element_type=jnp.float32)  9.47 us
    all_to_all x1, starting transfers between devices, body(): lax.all_to_all(partial_value, 'pool', split_axis=0, concat_axis=0, tiled=...  4.44 us
    reduce_scatter x1, waiting for transfers between devices, body(): lax.psum_scatter(mixed, 'tp', scatter_dimension=1, tiled=True)  4.24 us
    dot_general x1, matrix products, body(): jnp.dot(combining, gathered, precision=lax.Precision.HIGHEST, preferred_e...  3.25 us
  transfers between devices with their start and end apart: 2, of which 2 were waited for; matrix products, arithmetic and copies ran while one was open for 2% of the time, Pallas kernels for 0%

commit v1 on v0

v1 whole, which is shorter than its diff:
```python
import functools

import jax
import jax.numpy as jnp
from jax import lax
from jax.experimental import pallas as pl
from jax.experimental.pallas import tpu as pltpu
from jax.sharding import PartitionSpec as P

HDIM = 256
EXPERTS = 8
TOP = 3
MIB = 2**20
SWAP = [(0, 1), (1, 0)]
VMEM = pltpu.VMEM
BF16 = jnp.bfloat16
F32 = jnp.float32


def distances(count):
    pairs, top = [], count // 2
    while top >= 2:
        half = top // 2
        pairs += [(top + i, top + half + i) for i in range(half)]
        top //= 2
    return pairs


def route_of(count, pair):
    return [
        (p * 2 + c, (p ^ pair[c]) * 2 + c) for p in range(count) for c in range(2)
    ]


def attention(queries, keys, values, lengths):
    requests_here = queries.shape[0]
    heads_here = queries.shape[1] // HDIM
    query_heads = queries.reshape(requests_here, heads_here, HDIM)
    scores = jnp.einsum(
        "rhd,rkd->rhk", query_heads, keys, preferred_element_type=jnp.float32
    ) * HDIM ** (-0.5)
    live = jnp.arange(keys.shape[1], dtype=jnp.int32)[None, :] < lengths[:, None]
    scores = jnp.where(live[:, None, :], scores, -1e30)
    top = jnp.max(scores, axis=2, keepdims=True)
    weights = jnp.exp(scores - top)
    total = jnp.sum(weights, axis=2, keepdims=True)
    summed = jnp.einsum(
        "rhk,rkd->rhd", weights.astype(jnp.bfloat16), values, preferred_element_type=jnp.float32
    )
    return (summed / total).astype(jnp.bfloat16).reshape(requests_here, heads_here * HDIM)


def places(routes, levels, ks, span, capacity):
    rows = routes.shape[1]
    me = lax.axis_index("pool")
    slots = len(ks) * capacity
    slot = lax.broadcasted_iota(jnp.int32, (slots, 1), 0)
    expert = jnp.zeros((slots, 1), jnp.int32)
    for i, k in enumerate(ks):
        named = lax.bitwise_xor(me, k)
        if span > 1:
            named = lax.div(named, span)
        expert = jnp.where(slot >= i * capacity, named, expert)
    chosen = jnp.zeros((slots, rows), jnp.bool_)
    level = jnp.zeros((slots, rows), jnp.int32)
    for t in range(TOP):
        same = routes[t : t + 1, :] == expert
        chosen = jnp.logical_or(chosen, same)
        if levels is not None:
            level = level + jnp.where(same, levels[t : t + 1, :], 0)
    before = lax.broadcasted_iota(jnp.int32, (rows, rows), 0) < lax.broadcasted_iota(
        jnp.int32, (rows, rows), 1
    )
    rank = jnp.dot(
        jnp.where(chosen, 1.0, 0.0).astype(BF16),
        jnp.where(before, 1.0, 0.0).astype(BF16),
        preferred_element_type=F32,
    )
    place = lax.rem(slot, capacity).astype(F32)
    here = jnp.logical_and(chosen, rank == place)
    return here, level


def dispatch_kernel(pairs, span, capacity, routes_ref, x_ref, *outs):
    core = lax.axis_index("tp")
    half = x_ref.shape[1] // 2
    ks = [jnp.where(core == 0, a, b) for a, b in pairs] + [1, 0]
    here, _ = places(routes_ref[...], None, ks, span, capacity)
    picks = jnp.where(here, 1.0, 0.0).astype(BF16)
    m = len(pairs)
    full = jnp.dot(picks, x_ref[...], preferred_element_type=F32)
    for i in range(m):
        outs[i][...] = full[i * capacity : (i + 1) * capacity].astype(BF16)
    outs[m + 1][...] = full[(m + 1) * capacity :].astype(BF16)
    mine = x_ref[:, pl.ds(pl.multiple_of(core * half, 128), half)]
    outs[m][...] = jnp.dot(
        picks[m * capacity : (m + 1) * capacity], mine, preferred_element_type=F32
    ).astype(BF16)


def expert_kernel(m, capacity, *refs):
    blocks = refs[: 2 * m]
    share_mine, share_theirs, own, gate_hbm, up_hbm, down_hbm, keep, give = refs[2 * m : 2 * m + 8]
    x, gate_w, up_w, down_w, total, result, hidden, gate_sem, up_sem, down_sem = refs[2 * m + 8 :]
    core = lax.axis_index("tp")
    depth, width = gate_w.shape
    half = depth // 2
    steps, parts = gate_sem.shape[0], down_sem.shape[0]
    deep, wide = depth // steps, width // parts

    def fetch(source, target, sem, size, i):
        at = pl.ds(i * size, size)
        return pltpu.make_async_copy(source.at[at], target.at[at], sem.at[i])

    for i in range(steps):
        fetch(gate_hbm, gate_w, gate_sem, deep, i).start()
        fetch(up_hbm, up_w, up_sem, deep, i).start()
    for i in range(parts):
        fetch(down_hbm, down_w, down_sem, wide, i).start()
    two = 2 * capacity
    for i in range(m):
        x[i * two : (i + 1) * two, :] = jnp.concatenate(
            [blocks[2 * i][...], blocks[2 * i + 1][...]], axis=0
        )
    for c, part in ((core, share_mine), (1 - core, share_theirs)):
        at = pl.ds(pl.multiple_of(c * half, 128), half)
        x[m * two : (m + 1) * two, at] = jnp.concatenate([part[...], own[:, at]], axis=0)
    for i in range(steps):
        rows = x[:, i * deep : (i + 1) * deep]
        for j, (weight, source, sem) in enumerate(
            ((gate_w, gate_hbm, gate_sem), (up_w, up_hbm, up_sem))
        ):
            fetch(source, weight, sem, deep, i).wait()
            term = jnp.dot(
                rows, weight[i * deep : (i + 1) * deep, :], preferred_element_type=F32
            )
            total[j] = term if i == 0 else total[j] + term
    gate = total[0]
    hidden[...] = (gate / (1.0 + jnp.exp(-gate)) * total[1]).astype(BF16)
    for i in range(parts):
        fetch(down_hbm, down_w, down_sem, wide, i).wait()
        term = jnp.dot(
            hidden[:, i * wide : (i + 1) * wide],
            down_w[i * wide : (i + 1) * wide, :],
            preferred_element_type=F32,
        )
        result[...] = term if i == 0 else result[...] + term
    n = m * capacity
    keep[:n, :] = result[:n, :]
    mine = pl.ds(pl.multiple_of(core * half, 128), half)
    theirs = pl.ds(pl.multiple_of((1 - core) * half, 128), half)
    keep[n:, :half] = result[2 * n : 2 * n + capacity, mine]
    keep[n:, half:] = result[2 * n + capacity :, mine]
    rest = jnp.concatenate(
        [result[2 * n : 2 * n + capacity, theirs], result[2 * n + capacity :, theirs]], axis=1
    )
    give[...] = jnp.concatenate([result[n : 2 * n, :], rest], axis=0).astype(BF16)


def sum_kernel(m, capacity, keep, got, *outs):
    both = keep[...] + got[...].astype(F32)
    half = keep.shape[1] // 2
    for i in range(m):
        outs[i][...] = both[i * capacity : (i + 1) * capacity].astype(BF16)
    outs[m][...] = both[m * capacity :, :half].astype(BF16)
    outs[m + 1][...] = both[m * capacity :, half:].astype(BF16)


def combine_kernel(pairs, span, capacity, routes_ref, level_ref, *refs):
    m = len(pairs)
    blocks, shared, own, out = refs[: 2 * m], refs[2 * m], refs[2 * m + 1], refs[2 * m + 2]
    core = lax.axis_index("tp")
    half = out.shape[1]
    ks = [jnp.where(core == 0, a, b) for a, b in pairs]
    ks += [jnp.where(core == 0, b, a) for a, b in pairs] + [1, 0]
    here, level = places(routes_ref[...], level_ref[...], ks, span, capacity)
    weight = jnp.where(here, level, 0).astype(F32) / 1024.0
    high = weight.astype(BF16)
    low = (weight - high.astype(F32)).astype(BF16)
    at = pl.ds(pl.multiple_of(core * half, 128), half)
    held = jnp.concatenate([b[:, at] for b in blocks] + [shared[...], own[...]], axis=0)
    dims = (((0,), (0,)), ((), ()))
    out[...] = (
        lax.dot_general(high, held, dims, preferred_element_type=F32)
        + lax.dot_general(low, held, dims, preferred_element_type=F32)
    ).astype(BF16)


def body(queries, keys, values, lengths, moe_input, routes, gate_level, w_gate, w_up, w_down):
    count = lax.axis_size("pool")
    span = count // EXPERTS
    rows_here, width = moe_input.shape
    capacity = rows_here // 2
    half = width // 2
    hid = w_gate.shape[2]
    pairs = distances(count)
    m = len(pairs)
    axes = ("pool", "tp")
    routes_t, level_t = routes.T, gate_level.T

    block = jax.ShapeDtypeStruct((capacity, width), BF16)
    half_block = jax.ShapeDtypeStruct((capacity, half), BF16)
    in_vmem = pl.BlockSpec(memory_space=VMEM)
    *sent, shared, own = pl.pallas_call(
        functools.partial(dispatch_kernel, pairs, span, capacity),
        out_shape=[block] * m + [half_block, block],
        in_specs=[in_vmem] * 2,
        out_specs=[in_vmem] * (m + 2),
        compiler_params=pltpu.CompilerParams(vmem_limit_bytes=(12 if m < 8 else 40) * MIB),
        name="dispatch",
    )(routes_t, moe_input)

    mine = [lax.ppermute(b, axes, route_of(count, pair)) for b, pair in zip(sent, pairs)]
    share_mine = lax.ppermute(shared, axes, route_of(count, (1, 1)))
    theirs = [lax.ppermute(b, "tp", SWAP) for b in mine]
    share_theirs = lax.ppermute(share_mine, "tp", SWAP)

    context = attention(queries, keys, values, lengths)

    total_rows = count * capacity
    steps = 14
    parts = hid // 256 if hid % 256 == 0 else 1
    weight_bytes = 3 * width * hid * 2
    keep, give = pl.pallas_call(
        functools.partial(expert_kernel, m, capacity),
        out_shape=[
            jax.ShapeDtypeStruct(((m + 1) * capacity, width), F32),
            jax.ShapeDtypeStruct(((m + 1) * capacity, width), BF16),
        ],
        in_specs=[in_vmem] * (2 * m + 3) + [pl.BlockSpec(memory_space=pl.ANY)] * 3,
        out_specs=[in_vmem] * 2,
        scratch_shapes=[
            VMEM((total_rows, width), BF16),
            VMEM((width, hid), BF16),
            VMEM((width, hid), BF16),
            VMEM((hid, width), BF16),
            VMEM((2, total_rows, hid), F32),
            VMEM((total_rows, width), F32),
            VMEM((total_rows, hid), BF16),
            pltpu.SemaphoreType.DMA((steps,)),
            pltpu.SemaphoreType.DMA((steps,)),
            pltpu.SemaphoreType.DMA((parts,)),
        ],
        compiler_params=pltpu.CompilerParams(vmem_limit_bytes=60 * MIB),
        cost_estimate=pl.CostEstimate(
            flops=2 * total_rows * 3 * width * hid, bytes_accessed=weight_bytes, transcendentals=0
        ),
        name="experts",
    )(*mine, *theirs, share_mine, share_theirs, own, w_gate[0], w_up[0], w_down[0])

    got = lax.ppermute(give, "tp", SWAP)
    *back, share_back, own_back = pl.pallas_call(
        functools.partial(sum_kernel, m, capacity),
        out_shape=[block] * m + [half_block] * 2,
        in_specs=[in_vmem] * 2,
        out_specs=[in_vmem] * (m + 2),
        compiler_params=pltpu.CompilerParams(vmem_limit_bytes=(12 if m < 8 else 40) * MIB),
        name="sum",
    )(keep, got)

    mine = [lax.ppermute(b, axes, route_of(count, pair)) for b, pair in zip(back, pairs)]
    share_back = lax.ppermute(share_back, axes, route_of(count, (1, 1)))
    theirs = [lax.ppermute(b, "tp", SWAP) for b in mine]
    moe_output = pl.pallas_call(
        functools.partial(combine_kernel, pairs, span, capacity),
        out_shape=jax.ShapeDtypeStruct((rows_here, half), BF16),
        in_specs=[in_vmem] * (2 * m + 4),
        out_specs=in_vmem,
        compiler_params=pltpu.CompilerParams(vmem_limit_bytes=(12 if m < 8 else 40) * MIB),
        name="combine",
    )(routes_t, level_t, *mine, *theirs, share_back, own_back)
    return (context, moe_output)


def solution(mesh):
    return jax.shard_map(
        body,
        mesh=mesh,
        in_specs=(
            P(("group", "pool"), "tp"),
            P(("group", "pool"), None, None),
            P(("group", "pool"), None, None),
            P(("group", "pool")),
            P(("group", "pool"), None),
            P(("group", "pool"), None),
            P(("group", "pool"), None),
            P("pool", None, "tp"),
            P("pool", None, "tp"),
            P("pool", "tp", None),
        ),
        out_specs=(P(("group", "pool"), "tp"), P(("group", "pool"), "tp")),
        check_vma=False,
    )
```

time: 135 us -> 61.3 us (0.45)
  matrix products: 34.5 us -> 1.32 us
  blocking collectives: 30.4 us -> 0 us
  waiting for transfers between devices: 45.6 us -> 18.2 us
  Pallas kernels: 0 us -> 23.7 us
  between operations: 14.1 us -> 0.81 us
  starting transfers between devices: 4.48 us -> 13 us
  other arithmetic: 3.09 us -> 0.3 us
  local copies, waits for them, and re-layouts: 2.34 us -> 3.84 us
    all_to_all x1 -> x0, waiting for transfers between devices: 41.3 us -> none  [body(): lax.all_to_all(partial_value, 'pool', split_axis=0, concat_axis=0, tiled=...]
    dot_general x4 -> x0, matrix products: 33.1 us -> none  [the longest x1 19.1 us: body(): jnp.dot(hidden, w_down[0], preferred_element_type=jnp.float32)]
    all_to_all x1 -> x0, blocking collectives: 30.4 us -> none  [body(): lax.all_to_all(outgoing, 'pool', split_axis=0, concat_axis=0, tiled=True)]
    pallas_call x0 -> x4, Pallas kernels: none -> 23.7 us  [the longest x1 22.1 us: body(): pl.pallas_call(functools.partial(expert_kernel, m, capacity), out_shape=[...]
    ppermute x0 -> x16, waiting for transfers between devices: none -> 18.2 us  [the longest x6 15.9 us: body(): lax.ppermute(b, axes, route_of(count, pair))]
    ppermute x0 -> x16, starting transfers between devices: none -> 13 us  [the longest x6 10.2 us: body(): lax.ppermute(b, axes, route_of(count, pair))]
    all_to_all x1 -> x0, starting transfers between devices: 4.44 us -> none  [body(): lax.all_to_all(partial_value, 'pool', split_axis=0, concat_axis=0, tiled=...]
    reduce_scatter x1 -> x0, waiting for transfers between devices: 4.24 us -> none  [body(): lax.psum_scatter(mixed, 'tp', scatter_dimension=1, tiled=True)]
  transfers between devices with their start and end apart: 2 -> 16, of which waited for: 2 -> 8; matrix products, arithmetic and copies ran while one was open for 2% -> 4% of each run, Pallas kernels for 0% -> 0%
where the time goes in v1:
time: 61.3 us; the launch traced here: 61.2 us
  Pallas kernels  23.7 us (39%)
  waiting for transfers between devices  18.2 us (30%)
  starting transfers between devices  13 us (21%)
  local copies, waits for them, and re-layouts  3.84 us (6%)
  matrix products  1.32 us (2%)
  between operations  0.81 us (1%)
    pallas_call x1, Pallas kernels, body(): pl.pallas_call(functools.partial(expert_kernel, m, capacity), out_shape=[...  22.1 us
    ppermute x6, waiting for transfers between devices, body(): lax.ppermute(b, axes, route_of(count, pair))  15.9 us
    ppermute x6, starting transfers between devices, body(): lax.ppermute(b, axes, route_of(count, pair))  10.2 us
    unnamed x37, local copies, waits for them, and re-layouts  3.84 us
    ppermute x1, starting transfers between devices, body(): share_back = lax.ppermute(share_back, axes, route_of(count, (1, 1)))  1.48 us
  transfers between devices with their start and end apart: 16, of which 8 were waited for; matrix products, arithmetic and copies ran while one was open for 4% of the time, Pallas kernels for 0%

profile of v1, /device:TPU:0, one launch (start us, length us, event | category | flops | bytes accessed | tf_op | source)
XLA Modules:
  0.0 61.2 jit_solution(11721439056244991403)
XLA Ops:
  0.7 1.1 %copy-done.2 = bf16[16,7168]{1,0:T(8,128)(2,1)S(1)} copy-done((bf16[16,7168]{1,0:T(8,128)(2,1)S(1)}, bf16[16,7168]{1,0:T(8,128)(2,1)}, u32[]{:S(2)}) %copy-start.2) | copy-done | bytes 229400
  1.7 0.7 %copy-done.4 = s32[16,3]{0,1:T(4,128)S(1)} copy-done((s32[16,3]{0,1:T(4,128)S(1)}, s32[16,3]{0,1:T(4,128)}, u32[]{:S(2)}) %copy-start.4) | copy-done | bytes 216
  2.4 0.5 dispatch.1
  2.9 0.6 %copy-done.3 = bf16[8,7168]{1,0:T(8,128)(2,1)} copy-done((bf16[8,7168]{1,0:T(8,128)(2,1)}, bf16[8,7168]{1,0:T(8,128)(2,1)S(1)}, u32[]{:S(2)}) %copy-start.3) | copy-done | bytes 114712
  3.5 4.0 %collective-permute-start = (bf16[8,7168]{1,0:T(8,128)(2,1)S(1)}, bf16[8,7168]{1,0:T(8,128)(2,1)S(1)}, u32[]{:S(2)}, u32[]{:S(2)}) collective-permute-start(bf16[8,7168]{1,0:T(8,128)(2,1)S(1)} %get-tuple-element.14), channel_id=1, source_target_pairs={{0,8},{1,13},{2,10},{3,15},{4,12},{5,9},{6,14},{7,11},{8,0},{9,5},... | collective-permute-start | bytes 344072 | tf_op jit(solution)/shard_map/ppermute | solution.py:213
  7.6 1.3 %collective-permute-start.1 = (bf16[8,7168]{1,0:T(8,128)(2,1)S(1)}, bf16[8,7168]{1,0:T(8,128)(2,1)S(1)}, u32[]{:S(2)}, u32[]{:S(2)}) collective-permute-start(bf16[8,7168]{1,0:T(8,128)(2,1)S(1)} %get-tuple-element.15), channel_id=1, source_target_pairs={{0,10},{1,15},{2,8},{3,13},{4,14},{5,11},{6,12},{7,9},{8,2},{9,7},... | collective-permute-start | bytes 344072 | tf_op jit(solution)/shard_map/ppermute | solution.py:213
  8.8 1.6 %collective-permute-start.2 = (bf16[8,7168]{1,0:T(8,128)(2,1)S(1)}, bf16[8,7168]{1,0:T(8,128)(2,1)S(1)}, u32[]{:S(2)}, u32[]{:S(2)}) collective-permute-start(bf16[8,7168]{1,0:T(8,128)(2,1)S(1)} %get-tuple-element.16), channel_id=1, source_target_pairs={{0,4},{1,7},{2,6},{3,5},{4,0},{5,3},{6,2},{7,1},{8,12},{9,15},{10,... | collective-permute-start | bytes 344072 | tf_op jit(solution)/shard_map/ppermute | solution.py:213
  10.4 0.5 collective-permute-start.6
  10.9 5.5 %collective-permute-done.refs_0_ = bf16[8,7168]{1,0:T(8,128)(2,1)S(1)} collective-permute-done((bf16[8,7168]{1,0:T(8,128)(2,1)S(1)}, bf16[8,7168]{1,0:T(8,128)(2,1)S(1)}, u32[]{:S(2)}, u32[]{:S(2)}) %collective-permute-start) | collective-permute-done | bytes 114720 | tf_op jit(solution)/shard_map/ppermute | solution.py:213
  16.4 2.7 %collective-permute-done.1.refs_1_ = bf16[8,7168]{1,0:T(8,128)(2,1)S(1)} collective-permute-done((bf16[8,7168]{1,0:T(8,128)(2,1)S(1)}, bf16[8,7168]{1,0:T(8,128)(2,1)S(1)}, u32[]{:S(2)}, u32[]{:S(2)}) %collective-permute-start.1) | collective-permute-done | bytes 114720 | tf_op jit(solution)/shard_map/ppermute | solution.py:213
  19.2 0.5 collective-permute-start.5
  19.7 0.1 collective-permute-start.7
  19.8 1.2 %collective-permute-done.7.refs_7_ = bf16[8,3584]{1,0:T(8,128)(2,1)S(1)} collective-permute-done((bf16[8,3584]{1,0:T(8,128)(2,1)S(1)}, bf16[8,3584]{1,0:T(8,128)(2,1)S(1)}, u32[]{:S(2)}, u32[]{:S(2)}) %collective-permute-start.7) | collective-permute-done | bytes 57376 | tf_op jit(solution)/shard_map/ppermute | solution.py:216
  21.0 0.5 copy-done.16
  21.6 0.1 copy-done.12
  21.7 22.1 %experts.1 = (f32[32,7168]{1,0:T(8,128)}, bf16[32,7168]{1,0:T(8,128)(2,1)}) custom-call(bf16[8,7168]{1,0:T(8,128)(2,1)} %copy-done.8, bf16[8,7168]{1,0:T(8,128)(2,1)} %copy-done.9, bf16[8,7168]{1,0:T(8,128)(2,1)} %copy-done.10, bf16[8,7168]{1,0:T(8,128)(2,1)} %copy-done.11, bf16[8,7168]{1,0:T(8,128)(2,1)} %copy-done.12, bf16[8,7168]{1,0:T(8,128)(2,1)} %copy-done.13, ...), custom_call_target="tpu_custom_call" | custom-call | flops 3523215360 | bytes 55050240 | tf_op jit(solution)/shard_map/experts/pallas_call | solution.py:224
  43.8 0.2 collective-permute-start.8
  44.0 0.1 iota_compare_fusion
  44.1 0.8 %fusion.9 = (f32[4,32]{1,0:T(4,128)S(1)}, f32[4,32,1024]{2,1,0:T(8,128)S(1)}) fusion(bf16[4,1024,256]{2,1,0:T(8,128)(2,1)S(1)} %copy-done, bf16[1,4,32,256]{3,1,2,0:T(4,128)(2,1)S(1)} %bitcast.22, pred[4,1024]{1,0:T(4,128)(4,1)S(1)} %iota_compare_fusion), kind=kOutput, calls=%fused_computation.12 | convolution fusion | flops 67501952 | bytes 2691584 | tf_op jit(solution)/shard_map/rhd,rkd->rhk/dot_general | solution.py:39
  45.0 1.0 %collective-permute-done.8.got = bf16[32,7168]{1,0:T(8,128)(2,1)S(1)} collective-permute-done((bf16[32,7168]{1,0:T(8,128)(2,1)}, bf16[32,7168]{1,0:T(8,128)(2,1)S(1)}, u32[]{:S(2)}, u32[]{:S(2)}) %collective-permute-start.8) | collective-permute-done | bytes 458784 | tf_op jit(solution)/shard_map/ppermute | solution.py:251
  45.9 0.1 sum.1
  46.1 2.9 %collective-permute-start.10 = (bf16[8,7168]{1,0:T(8,128)(2,1)S(1)}, bf16[8,7168]{1,0:T(8,128)(2,1)S(1)}, u32[]{:S(2)}, u32[]{:S(2)}) collective-permute-start(bf16[8,7168]{1,0:T(8,128)(2,1)S(1)} %get-tuple-element.22), channel_id=1, source_target_pairs={{0,10},{1,15},{2,8},{3,13},{4,14},{5,11},{6,12},{7,9},{8,2},{9,7},... | collective-permute-start | bytes 344072 | tf_op jit(solution)/shard_map/ppermute | solution.py:261
  49.0 0.4 collective-permute-start.11
  49.3 0.2 fusion.3
  49.6 1.5 %collective-permute-start.15 = (bf16[8,3584]{1,0:T(8,128)(2,1)S(1)}, bf16[8,3584]{1,0:T(8,128)(2,1)S(1)}, u32[]{:S(2)}, u32[]{:S(2)}) collective-permute-start(bf16[8,3584]{1,0:T(8,128)(2,1)S(1)} %get-tuple-element.24), channel_id=1, source_target_pairs={{0,2},{1,3},{2,0},{3,1},{4,6},{5,7},{6,4},{7,5},{8,10},{9,11},{10,... | collective-permute-start | bytes 172040 | tf_op jit(solution)/shard_map/ppermute | solution.py:262
  51.0 5.6 %collective-permute-done.9.refs_0_ = bf16[8,7168]{1,0:T(8,128)(2,1)S(1)} collective-permute-done((bf16[8,7168]{1,0:T(8,128)(2,1)S(1)}, bf16[8,7168]{1,0:T(8,128)(2,1)S(1)}, u32[]{:S(2)}, u32[]{:S(2)}) %collective-permute-start.9) | collective-permute-done | bytes 114720 | tf_op jit(solution)/shard_map/ppermute | solution.py:261
  56.7 1.5 %collective-permute-done.10.refs_1_ = bf16[8,7168]{1,0:T(8,128)(2,1)S(1)} collective-permute-done((bf16[8,7168]{1,0:T(8,128)(2,1)S(1)}, bf16[8,7168]{1,0:T(8,128)(2,1)S(1)}, u32[]{:S(2)}, u32[]{:S(2)}) %collective-permute-start.10) | collective-permute-done | bytes 114720 | tf_op jit(solution)/shard_map/ppermute | solution.py:261
  58.2 0.6 collective-permute-done.11.refs_2_
  58.8 0.5 fusion.2
  59.3 0.7 %copy.13 = bf16[1,4,32,256]{3,1,2,0:T(4,128)(2,1)} copy(bf16[1,4,32,256]{3,2,1,0:T(8,128)(2,1)S(1)} %fusion.2) | data formatting | bytes 131072
  60.0 0.1 collective-permute-done.14.refs_5_
  60.1 1.1 %combine.1 = bf16[16,3584]{1,0:T(8,128)(2,1)} custom-call(s32[3,16]{1,0:T(4,128)S(1)} %bitcast.17, s32[3,16]{1,0:T(4,128)S(1)} %bitcast.18, bf16[8,7168]{1,0:T(8,128)(2,1)S(1)} %collective-permute-done.9.refs_0_, bf16[8,7168]{1,0:T(8,128)(2,1)S(1)} %collective-permute-done.10.refs_1_, bf16[8,7168]{1,0:T(8,128)(2,1)S(1)} %collective-permute-done.11.refs_2_, ...), custom_call_target="tpu_custom_call" | custom-call | tf_op jit(solution)/shard_map/combine/pallas_call | solution.py:264
  (45 shorter events, 0.2 us)
Async XLA Ops:
  0.6 43.5 %copy-start = (bf16[4,1024,256]{2,1,0:T(8,128)(2,1)S(1)}, bf16[4,1024,256]{2,1,0:T(8,128)(2,1)}, u32[]{:S(2)}) copy-start(bf16[4,1024,256]{2,1,0:T(8,128)(2,1)} %param.11) | copy-start | bytes 6291460
  0.6 1.1 %copy-start.2 = (bf16[16,7168]{1,0:T(8,128)(2,1)S(1)}, bf16[16,7168]{1,0:T(8,128)(2,1)}, u32[]{:S(2)}) copy-start(bf16[16,7168]{1,0:T(8,128)(2,1)} %x_ref.1) | copy-start | bytes 688132
  1.7 0.7 %copy-start.4 = (s32[16,3]{0,1:T(4,128)S(1)}, s32[16,3]{0,1:T(4,128)}, u32[]{:S(2)}) copy-start(s32[16,3]{0,1:T(4,128)} %param.15) | copy-start | bytes 580
  3.5 12.9 %collective-permute-start = (bf16[8,7168]{1,0:T(8,128)(2,1)S(1)}, bf16[8,7168]{1,0:T(8,128)(2,1)S(1)}, u32[]{:S(2)}, u32[]{:S(2)}) collective-permute-start(bf16[8,7168]{1,0:T(8,128)(2,1)S(1)} %get-tuple-element.14), channel_id=1, source_target_pairs={{0,8},{1,13},{2,10},{3,15},{4,12},{5,9},{6,14},{7,11},{8,0},{9,5},... | collective-permute-start | bytes 344072 | tf_op jit(solution)/shard_map/ppermute | solution.py:213
  7.6 11.6 %collective-permute-start.1 = (bf16[8,7168]{1,0:T(8,128)(2,1)S(1)}, bf16[8,7168]{1,0:T(8,128)(2,1)S(1)}, u32[]{:S(2)}, u32[]{:S(2)}) collective-permute-start(bf16[8,7168]{1,0:T(8,128)(2,1)S(1)} %get-tuple-element.15), channel_id=1, source_target_pairs={{0,10},{1,15},{2,8},{3,13},{4,14},{5,11},{6,12},{7,9},{8,2},{9,7},... | collective-permute-start | bytes 344072 | tf_op jit(solution)/shard_map/ppermute | solution.py:213
  8.8 10.4 %collective-permute-start.2 = (bf16[8,7168]{1,0:T(8,128)(2,1)S(1)}, bf16[8,7168]{1,0:T(8,128)(2,1)S(1)}, u32[]{:S(2)}, u32[]{:S(2)}) collective-permute-start(bf16[8,7168]{1,0:T(8,128)(2,1)S(1)} %get-tuple-element.16), channel_id=1, source_target_pairs={{0,4},{1,7},{2,6},{3,5},{4,0},{5,3},{6,2},{7,1},{8,12},{9,15},{10,... | collective-permute-start | bytes 344072 | tf_op jit(solution)/shard_map/ppermute | solution.py:213
  10.4 9.3 %collective-permute-start.6 = (bf16[8,3584]{1,0:T(8,128)(2,1)S(1)}, bf16[8,3584]{1,0:T(8,128)(2,1)S(1)}, u32[]{:S(2)}, u32[]{:S(2)}) collective-permute-start(bf16[8,3584]{1,0:T(8,128)(2,1)S(1)} %get-tuple-element.17), channel_id=1, source_target_pairs={{0,2},{1,3},{2,0},{3,1},{4,6},{5,7},{6,4},{7,5},{8,10},{9,11},{10,... | collective-permute-start | bytes 172040 | tf_op jit(solution)/shard_map/ppermute | solution.py:214
  16.4 4.6 %copy-start.8 = (bf16[8,7168]{1,0:T(8,128)(2,1)}, bf16[8,7168]{1,0:T(8,128)(2,1)S(1)}, u32[]{:S(2)}) copy-start(bf16[8,7168]{1,0:T(8,128)(2,1)S(1)} %collective-permute-done.refs_0_) | copy-start | bytes 344068
  16.4 4.5 %collective-permute-start.3 = (bf16[8,7168]{1,0:T(8,128)(2,1)S(1)}, bf16[8,7168]{1,0:T(8,128)(2,1)S(1)}, u32[]{:S(2)}, u32[]{:S(2)}) collective-permute-start(bf16[8,7168]{1,0:T(8,128)(2,1)S(1)} %collective-permute-done.refs_0_), channel_id=1, source_target_pairs={{0,1},{1,0},{2,3},{3,2},{4,5},{5,4},{6,7},{7,6},{8,9},{9,8},{10,11... | collective-permute-start | bytes 344072 | tf_op jit(solution)/shard_map/ppermute | solution.py:215
  19.2 1.8 %copy-start.9 = (bf16[8,7168]{1,0:T(8,128)(2,1)}, bf16[8,7168]{1,0:T(8,128)(2,1)S(1)}, u32[]{:S(2)}) copy-start(bf16[8,7168]{1,0:T(8,128)(2,1)S(1)} %collective-permute-done.1.refs_1_) | copy-start | bytes 344068
  19.2 1.8 %collective-permute-start.4 = (bf16[8,7168]{1,0:T(8,128)(2,1)S(1)}, bf16[8,7168]{1,0:T(8,128)(2,1)S(1)}, u32[]{:S(2)}, u32[]{:S(2)}) collective-permute-start(bf16[8,7168]{1,0:T(8,128)(2,1)S(1)} %collective-permute-done.1.refs_1_), channel_id=1, source_target_pairs={{0,1},{1,0},{2,3},{3,2},{4,5},{5,4},{6,7},{7,6},{8,9},{9,8},{10,11... | collective-permute-start | bytes 344072 | tf_op jit(solution)/shard_map/ppermute | solution.py:215
  19.2 1.8 %copy-start.10 = (bf16[8,7168]{1,0:T(8,128)(2,1)}, bf16[8,7168]{1,0:T(8,128)(2,1)S(1)}, u32[]{:S(2)}) copy-start(bf16[8,7168]{1,0:T(8,128)(2,1)S(1)} %collective-permute-done.2.refs_2_) | copy-start | bytes 344068
  19.2 1.8 %collective-permute-start.5 = (bf16[8,7168]{1,0:T(8,128)(2,1)S(1)}, bf16[8,7168]{1,0:T(8,128)(2,1)S(1)}, u32[]{:S(2)}, u32[]{:S(2)}) collective-permute-start(bf16[8,7168]{1,0:T(8,128)(2,1)S(1)} %collective-permute-done.2.refs_2_), channel_id=1, source_target_pairs={{0,1},{1,0},{2,3},{3,2},{4,5},{5,4},{6,7},{7,6},{8,9},{9,8},{10,11... | collective-permute-start | bytes 344072 | tf_op jit(solution)/shard_map/ppermute | solution.py:215
  19.7 1.3 %copy-start.15 = (bf16[8,3584]{1,0:T(8,128)(2,1)}, bf16[8,3584]{1,0:T(8,128)(2,1)S(1)}, u32[]{:S(2)}) copy-start(bf16[8,3584]{1,0:T(8,128)(2,1)S(1)} %collective-permute-done.6.refs_6_) | copy-start | bytes 172036
  19.7 1.2 %collective-permute-start.7 = (bf16[8,3584]{1,0:T(8,128)(2,1)S(1)}, bf16[8,3584]{1,0:T(8,128)(2,1)S(1)}, u32[]{:S(2)}, u32[]{:S(2)}) collective-permute-start(bf16[8,3584]{1,0:T(8,128)(2,1)S(1)} %collective-permute-done.6.refs_6_), channel_id=1, source_target_pairs={{0,1},{1,0},{2,3},{3,2},{4,5},{5,4},{6,7},{7,6},{8,9},{9,8},{10,11... | collective-permute-start | bytes 172040 | tf_op jit(solution)/shard_map/ppermute | solution.py:216
  21.0 0.7 %copy-start.11 = (bf16[8,7168]{1,0:T(8,128)(2,1)}, bf16[8,7168]{1,0:T(8,128)(2,1)S(1)}, u32[]{:S(2)}) copy-start(bf16[8,7168]{1,0:T(8,128)(2,1)S(1)} %collective-permute-done.3.refs_3_) | copy-start | bytes 344068
  21.0 0.7 %copy-start.12 = (bf16[8,7168]{1,0:T(8,128)(2,1)}, bf16[8,7168]{1,0:T(8,128)(2,1)S(1)}, u32[]{:S(2)}) copy-start(bf16[8,7168]{1,0:T(8,128)(2,1)S(1)} %collective-permute-done.4.refs_4_) | copy-start | bytes 344068
  21.0 0.7 %copy-start.13 = (bf16[8,7168]{1,0:T(8,128)(2,1)}, bf16[8,7168]{1,0:T(8,128)(2,1)S(1)}, u32[]{:S(2)}) copy-start(bf16[8,7168]{1,0:T(8,128)(2,1)S(1)} %collective-permute-done.5.refs_5_) | copy-start | bytes 344068
  21.7 22.3 %copy-start.17 = (s32[4]{0:T(128)S(1)}, s32[4]{0:T(128)}, u32[]{:S(2)}) copy-start(s32[4]{0:T(128)} %param.13) | copy-start | bytes 52
  21.7 22.4 %copy-start.14 = (bf16[4,8192]{1,0:T(4,128)(2,1)S(1)}, bf16[4,8192]{1,0:T(4,128)(2,1)}, u32[]{:S(2)}) copy-start(bf16[4,8192]{1,0:T(4,128)(2,1)} %param.10) | copy-start | bytes 196612
  43.8 2.1 %copy-start.1 = (f32[32,7168]{1,0:T(8,128)S(1)}, f32[32,7168]{1,0:T(8,128)}, u32[]{:S(2)}) copy-start(f32[32,7168]{1,0:T(8,128)} %get-tuple-element.19.keep) | copy-start | bytes 2752516
  43.8 2.1 %collective-permute-start.8 = (bf16[32,7168]{1,0:T(8,128)(2,1)}, bf16[32,7168]{1,0:T(8,128)(2,1)S(1)}, u32[]{:S(2)}, u32[]{:S(2)}) collective-permute-start(bf16[32,7168]{1,0:T(8,128)(2,1)} %get-tuple-element.20), channel_id=1, source_target_pairs={{0,1},{1,0},{2,3},{3,2},{4,5},{5,4},{6,7},{7,6},{8,9},{9,8},{10,11... | collective-permute-start | bytes 1376264 | tf_op jit(solution)/shard_map/ppermute | solution.py:251
  44.1 14.6 %copy-start.7 = (bf16[4,1024,256]{2,1,0:T(8,128)(2,1)S(1)}, bf16[4,1024,256]{2,1,0:T(8,128)(2,1)}, u32[]{:S(2)}) copy-start(bf16[4,1024,256]{2,1,0:T(8,128)(2,1)} %param.12) | copy-start | bytes 6291460
  45.9 14.2 %copy-start.5 = (s32[16,3]{0,1:T(4,128)S(1)}, s32[16,3]{0,1:T(4,128)}, u32[]{:S(2)}) copy-start(s32[16,3]{0,1:T(4,128)} %param.15) | copy-start | bytes 580
  45.9 14.2 %copy-start.6 = (s32[16,3]{0,1:T(4,128)S(1)}, s32[16,3]{0,1:T(4,128)}, u32[]{:S(2)}) copy-start(s32[16,3]{0,1:T(4,128)} %param.16) | copy-start | bytes 580
  46.0 10.7 %collective-permute-start.9 = (bf16[8,7168]{1,0:T(8,128)(2,1)S(1)}, bf16[8,7168]{1,0:T(8,128)(2,1)S(1)}, u32[]{:S(2)}, u32[]{:S(2)}) collective-permute-start(bf16[8,7168]{1,0:T(8,128)(2,1)S(1)} %get-tuple-element.21), channel_id=1, source_target_pairs={{0,8},{1,13},{2,10},{3,15},{4,12},{5,9},{6,14},{7,11},{8,0},{9,5},... | collective-permute-start | bytes 344072 | tf_op jit(solution)/shard_map/ppermute | solution.py:261
  46.1 12.1 %collective-permute-start.10 = (bf16[8,7168]{1,0:T(8,128)(2,1)S(1)}, bf16[8,7168]{1,0:T(8,128)(2,1)S(1)}, u32[]{:S(2)}, u32[]{:S(2)}) collective-permute-start(bf16[8,7168]{1,0:T(8,128)(2,1)S(1)} %get-tuple-element.22), channel_id=1, source_target_pairs={{0,10},{1,15},{2,8},{3,13},{4,14},{5,11},{6,12},{7,9},{8,2},{9,7},... | collective-permute-start | bytes 344072 | tf_op jit(solution)/shard_map/ppermute | solution.py:261
  49.0 9.8 %collective-permute-start.11 = (bf16[8,7168]{1,0:T(8,128)(2,1)S(1)}, bf16[8,7168]{1,0:T(8,128)(2,1)S(1)}, u32[]{:S(2)}, u32[]{:S(2)}) collective-permute-start(bf16[8,7168]{1,0:T(8,128)(2,1)S(1)} %get-tuple-element.23), channel_id=1, source_target_pairs={{0,4},{1,7},{2,6},{3,5},{4,0},{5,3},{6,2},{7,1},{8,12},{9,15},{10,... | collective-permute-start | bytes 344072 | tf_op jit(solution)/shard_map/ppermute | solution.py:261
  49.6 10.4 %collective-permute-start.15 = (bf16[8,3584]{1,0:T(8,128)(2,1)S(1)}, bf16[8,3584]{1,0:T(8,128)(2,1)S(1)}, u32[]{:S(2)}, u32[]{:S(2)}) collective-permute-start(bf16[8,3584]{1,0:T(8,128)(2,1)S(1)} %get-tuple-element.24), channel_id=1, source_target_pairs={{0,2},{1,3},{2,0},{3,1},{4,6},{5,7},{6,4},{7,5},{8,10},{9,11},{10,... | collective-permute-start | bytes 172040 | tf_op jit(solution)/shard_map/ppermute | solution.py:262
  56.7 3.3 %collective-permute-start.12 = (bf16[8,7168]{1,0:T(8,128)(2,1)S(1)}, bf16[8,7168]{1,0:T(8,128)(2,1)S(1)}, u32[]{:S(2)}, u32[]{:S(2)}) collective-permute-start(bf16[8,7168]{1,0:T(8,128)(2,1)S(1)} %collective-permute-done.9.refs_0_), channel_id=1, source_target_pairs={{0,1},{1,0},{2,3},{3,2},{4,5},{5,4},{6,7},{7,6},{8,9},{9,8},{10,11... | collective-permute-start | bytes 344072 | tf_op jit(solution)/shard_map/ppermute | solution.py:263
  58.2 1.8 %collective-permute-start.13 = (bf16[8,7168]{1,0:T(8,128)(2,1)S(1)}, bf16[8,7168]{1,0:T(8,128)(2,1)S(1)}, u32[]{:S(2)}, u32[]{:S(2)}) collective-permute-start(bf16[8,7168]{1,0:T(8,128)(2,1)S(1)} %collective-permute-done.10.refs_1_), channel_id=1, source_target_pairs={{0,1},{1,0},{2,3},{3,2},{4,5},{5,4},{6,7},{7,6},{8,9},{9,8},{10,11... | collective-permute-start | bytes 344072 | tf_op jit(solution)/shard_map/ppermute | solution.py:263
  58.8 1.3 %collective-permute-start.14 = (bf16[8,7168]{1,0:T(8,128)(2,1)S(1)}, bf16[8,7168]{1,0:T(8,128)(2,1)S(1)}, u32[]{:S(2)}, u32[]{:S(2)}) collective-permute-start(bf16[8,7168]{1,0:T(8,128)(2,1)S(1)} %collective-permute-done.11.refs_2_), channel_id=1, source_target_pairs={{0,1},{1,0},{2,3},{3,2},{4,5},{5,4},{6,7},{7,6},{8,9},{9,8},{10,11... | collective-permute-start | bytes 344072 | tf_op jit(solution)/shard_map/ppermute | solution.py:263
  (2 other events, 1.3 us)

commit v2 on v1

--- a/solution.py
+++ b/solution.py
@@ -11,6 +11,7 @@
 EXPERTS = 8
 TOP = 3
 MIB = 2**20
+HEAD = 1024
 SWAP = [(0, 1), (1, 0)]
 VMEM = pltpu.VMEM
 BF16 = jnp.bfloat16
@@ -32,22 +33,55 @@
     ]
 
 
-def attention(queries, keys, values, lengths):
-    requests_here = queries.shape[0]
-    heads_here = queries.shape[1] // HDIM
-    query_heads = queries.reshape(requests_here, heads_here, HDIM)
-    scores = jnp.einsum(
-        "rhd,rkd->rhk", query_heads, keys, preferred_element_type=jnp.float32
-    ) * HDIM ** (-0.5)
-    live = jnp.arange(keys.shape[1], dtype=jnp.int32)[None, :] < lengths[:, None]
-    scores = jnp.where(live[:, None, :], scores, -1e30)
-    top = jnp.max(scores, axis=2, keepdims=True)
-    weights = jnp.exp(scores - top)
-    total = jnp.sum(weights, axis=2, keepdims=True)
-    summed = jnp.einsum(
-        "rhk,rkd->rhd", weights.astype(jnp.bfloat16), values, preferred_element_type=jnp.float32
-    )
-    return (summed / total).astype(jnp.bfloat16).reshape(requests_here, heads_here * HDIM)
+def attention_kernel(loads, *refs):
+    n = len(loads)
+    sources, weights, out_ref, held = refs[:4], refs[4:6], refs[6], refs[7 : 7 + n]
+    lengths_ref, q_ref, k_ref, v_ref, packed, mixed, own_sems, sems = refs[7 + n :]
+    own = [
+        pltpu.make_async_copy(source, ref, own_sems.at[i])
+        for i, (source, ref) in enumerate(zip(sources, (lengths_ref, q_ref, k_ref, v_ref)))
+    ]
+    for copy in own:
+        copy.start()
+    copies = []
+    for i, (which, start, rows) in enumerate(loads):
+        copy = pltpu.make_async_copy(
+            weights[which].at[pl.ds(start, rows)], held[i], sems.at[i]
+        )
+        copy.start()
+        copies.append(copy)
+    requests, slots, size = k_ref.shape
+    heads = q_ref.shape[1] // size
+    planes = packed.shape[0]
+    own[0].wait()
+    own[1].wait()
+    for i in range(heads * planes):
+        h, j = divmod(i, planes)
+        packed[j, h * requests : (h + 1) * requests, :] = q_ref[:, i * 128 : (i + 1) * 128].astype(
+            F32
+        )
+    own[2].wait()
+    own[3].wait()
+    for r in range(requests):
+        every = pl.ds(r, heads, stride=requests)
+        query = jnp.concatenate([packed[j, every, :] for j in range(planes)], axis=1).astype(BF16)
+        scores = lax.dot_general(
+            query, k_ref[r], (((1,), (1,)), ((), ())), preferred_element_type=F32
+        ) * size ** (-0.5)
+        live = lax.broadcasted_iota(jnp.int32, (1, slots), 1) < lengths_ref[r]
+        scores = jnp.where(live, scores, -1e30)
+        weight = jnp.exp(scores - jnp.max(scores, axis=1, keepdims=True))
+        total = jnp.sum(weight, axis=1, keepdims=True)
+        result = jnp.dot(weight.astype(BF16), v_ref[r], preferred_element_type=F32) / total
+        for j in range(planes):
+            mixed[j, every, :] = result[:, j * 128 : (j + 1) * 128]
+    for i in range(heads * planes):
+        h, j = divmod(i, planes)
+        out_ref[:, i * 128 : (i + 1) * 128] = mixed[
+            j, h * requests : (h + 1) * requests, :
+        ].astype(BF16)
+    for copy in copies:
+        copy.wait()
 
 
 def places(routes, levels, ks, span, capacity):
@@ -81,13 +115,20 @@
     return here, level
 
 
-def dispatch_kernel(pairs, span, capacity, routes_ref, x_ref, *outs):
+def dispatch_kernel(pairs, span, capacity, routes_hbm, x_hbm, *refs):
+    *outs, routes_ref, x_ref, sems = refs
+    get_routes = pltpu.make_async_copy(routes_hbm, routes_ref, sems.at[0])
+    get_x = pltpu.make_async_copy(x_hbm, x_ref, sems.at[1])
+    get_routes.start()
+    get_x.start()
+    get_routes.wait()
     core = lax.axis_index("tp")
     half = x_ref.shape[1] // 2
     ks = [jnp.where(core == 0, a, b) for a, b in pairs] + [1, 0]
     here, _ = places(routes_ref[...], None, ks, span, capacity)
     picks = jnp.where(here, 1.0, 0.0).astype(BF16)
     m = len(pairs)
+    get_x.wait()
     full = jnp.dot(picks, x_ref[...], preferred_element_type=F32)
     for i in range(m):
         outs[i][...] = full[i * capacity : (i + 1) * capacity].astype(BF16)
@@ -98,25 +139,43 @@
     ).astype(BF16)
 
 
-def expert_kernel(m, capacity, *refs):
+def expert_kernel(m, capacity, plan, *refs):
     blocks = refs[: 2 * m]
-    share_mine, share_theirs, own, gate_hbm, up_hbm, down_hbm, keep, give = refs[2 * m : 2 * m + 8]
-    x, gate_w, up_w, down_w, total, result, hidden, gate_sem, up_sem, down_sem = refs[2 * m + 8 :]
+    share_mine, share_theirs, own = refs[2 * m : 2 * m + 3]
+    held = sum(i >= 0 for ranges in plan for _, _, i in ranges)
+    at = 2 * m + 3
+    parts_held, refs = refs[at : at + held], refs[at + held :]
+    gate_hbm, up_hbm, down_hbm, keep, give = refs[:5]
+    x, rest_w, down_w, total, result, hidden, rest_sem, down_sem = refs[5:]
     core = lax.axis_index("tp")
-    depth, width = gate_w.shape
+    depth, width = x.shape[1], hidden.shape[1]
     half = depth // 2
-    steps, parts = gate_sem.shape[0], down_sem.shape[0]
-    deep, wide = depth // steps, width // parts
-
-    def fetch(source, target, sem, size, i):
-        at = pl.ds(i * size, size)
-        return pltpu.make_async_copy(source.at[at], target.at[at], sem.at[i])
-
-    for i in range(steps):
-        fetch(gate_hbm, gate_w, gate_sem, deep, i).start()
-        fetch(up_hbm, up_w, up_sem, deep, i).start()
-    for i in range(parts):
-        fetch(down_hbm, down_w, down_sem, wide, i).start()
+    wide, ring = down_w.shape[1], down_w.shape[0]
+    parts = width // wide
+
+    fetches, place = {}, 0
+    for j, (ranges, source) in enumerate(zip(plan, (gate_hbm, up_hbm))):
+        for start, rows, i in ranges:
+            if i < 0:
+                fetches[j, start] = (
+                    place,
+                    pltpu.make_async_copy(
+                        source.at[pl.ds(start, rows)],
+                        rest_w.at[pl.ds(place, rows)],
+                        rest_sem.at[len(fetches)],
+                    ),
+                )
+                place += rows
+    for _, copy in fetches.values():
+        copy.start()
+
+    def fetch(i):
+        return pltpu.make_async_copy(
+            down_hbm.at[pl.ds(i * wide, wide)], down_w.at[i % ring], down_sem.at[i]
+        )
+
+    for i in range(min(ring, parts)):
+        fetch(i).start()
     two = 2 * capacity
     for i in range(m):
         x[i * two : (i + 1) * two, :] = jnp.concatenate(
@@ -125,26 +184,26 @@
     for c, part in ((core, share_mine), (1 - core, share_theirs)):
         at = pl.ds(pl.multiple_of(c * half, 128), half)
         x[m * two : (m + 1) * two, at] = jnp.concatenate([part[...], own[:, at]], axis=0)
-    for i in range(steps):
-        rows = x[:, i * deep : (i + 1) * deep]
-        for j, (weight, source, sem) in enumerate(
-            ((gate_w, gate_hbm, gate_sem), (up_w, up_hbm, up_sem))
-        ):
-            fetch(source, weight, sem, deep, i).wait()
-            term = jnp.dot(
-                rows, weight[i * deep : (i + 1) * deep, :], preferred_element_type=F32
-            )
-            total[j] = term if i == 0 else total[j] + term
+    for j, ranges in enumerate(plan):
+        for start, rows, i in ranges:
+            if i < 0:
+                place, copy = fetches[j, start]
+                copy.wait()
+                weight = rest_w[place : place + rows, :]
+            else:
+                weight = parts_held[i][...]
+            term = jnp.dot(x[:, start : start + rows], weight, preferred_element_type=F32)
+            total[j] = term if start == 0 else total[j] + term
     gate = total[0]
     hidden[...] = (gate / (1.0 + jnp.exp(-gate)) * total[1]).astype(BF16)
     for i in range(parts):
-        fetch(down_hbm, down_w, down_sem, wide, i).wait()
+        fetch(i).wait()
         term = jnp.dot(
-            hidden[:, i * wide : (i + 1) * wide],
-            down_w[i * wide : (i + 1) * wide, :],
-            preferred_element_type=F32,
+            hidden[:, i * wide : (i + 1) * wide], down_w[i % ring], preferred_element_type=F32
         )
         result[...] = term if i == 0 else result[...] + term
+        if i + ring < parts:
+            fetch(i + ring).start()
     n = m * capacity
     keep[:n, :] = result[:n, :]
     mine = pl.ds(pl.multiple_of(core * half, 128), half)
@@ -197,6 +256,7 @@
     m = len(pairs)
     axes = ("pool", "tp")
     routes_t, level_t = routes.T, gate_level.T
+    far = functools.partial(pltpu.with_memory_space_constraint, memory_space=pltpu.HBM)
 
     block = jax.ShapeDtypeStruct((capacity, width), BF16)
     half_block = jax.ShapeDtypeStruct((capacity, half), BF16)
@@ -204,49 +264,93 @@
     *sent, shared, own = pl.pallas_call(
         functools.partial(dispatch_kernel, pairs, span, capacity),
         out_shape=[block] * m + [half_block, block],
-        in_specs=[in_vmem] * 2,
+        in_specs=[pl.BlockSpec(memory_space=pltpu.HBM)] * 2,
         out_specs=[in_vmem] * (m + 2),
-        compiler_params=pltpu.CompilerParams(vmem_limit_bytes=(12 if m < 8 else 40) * MIB),
+        scratch_shapes=[
+            VMEM(routes_t.shape, jnp.int32),
+            VMEM(moe_input.shape, BF16),
+            pltpu.SemaphoreType.DMA((2,)),
+        ],
+        compiler_params=pltpu.CompilerParams(vmem_limit_bytes=(8 if m < 8 else 40) * MIB),
         name="dispatch",
-    )(routes_t, moe_input)
+    )(far(routes_t), far(moe_input))
 
     mine = [lax.ppermute(b, axes, route_of(count, pair)) for b, pair in zip(sent, pairs)]
     share_mine = lax.ppermute(shared, axes, route_of(count, (1, 1)))
+    total_rows = count * capacity
+    step = width // 14
+    roomy = total_rows <= 64
+    loads, plan = [], ([], [])
+    for j, early in enumerate((width, HEAD) if roomy else (0, 0)):
+        for start in range(0, width, step):
+            index = -1
+            if start < early:
+                index = len(loads)
+                loads.append((j, start, step))
+            plan[j].append((start, step, index))
+    gate_hbm, up_hbm, down_hbm = (far(w[0]) for w in (w_gate, w_up, w_down))
+    requests, slots, size = keys.shape
+    heads = queries.shape[1] // size
+    in_hbm = pl.BlockSpec(memory_space=pltpu.HBM)
+    early_bytes = 4 * requests * slots * size + 2 * hid * step * len(loads)
+    context, *held = pl.pallas_call(
+        functools.partial(attention_kernel, loads),
+        out_shape=[jax.ShapeDtypeStruct(queries.shape, BF16)]
+        + [VMEM((rows, hid), BF16) for _, _, rows in loads],
+        in_specs=[in_hbm] * 6,
+        out_specs=[in_vmem] * (1 + len(loads)),
+        scratch_shapes=[
+            pltpu.SMEM(lengths.shape, jnp.int32),
+            VMEM(queries.shape, BF16),
+            VMEM(keys.shape, BF16),
+            VMEM(values.shape, BF16),
+            VMEM((size // 128, heads * requests, 128), F32),
+            VMEM((size // 128, heads * requests, 128), F32),
+            pltpu.SemaphoreType.DMA((4,)),
+            pltpu.SemaphoreType.DMA((max(1, len(loads)),)),
+        ],
+        compiler_params=pltpu.CompilerParams(vmem_limit_bytes=10 * MIB),
+        cost_estimate=pl.CostEstimate(
+            flops=4 * requests * heads * slots * size,
+            bytes_accessed=early_bytes,
+            transcendentals=requests * heads * slots,
+        ),
+        name="attention",
+    )(far(lengths), far(queries), far(keys), far(values), gate_hbm, up_hbm)
+
+    *mine, share_mine, context = lax.optimization_barrier((*mine, share_mine, context))
     theirs = [lax.ppermute(b, "tp", SWAP) for b in mine]
     share_theirs = lax.ppermute(share_mine, "tp", SWAP)
 
-    context = attention(queries, keys, values, lengths)
-
-    total_rows = count * capacity
-    steps = 14
-    parts = hid // 256 if hid % 256 == 0 else 1
-    weight_bytes = 3 * width * hid * 2
+    fetched = 2 * 14 - len(loads)
+    wide = 256 if hid % 256 == 0 else hid
+    parts = hid // wide
+    ring = min(parts, 3)
+    weight_bytes = 2 * hid * (step * fetched + width)
     keep, give = pl.pallas_call(
-        functools.partial(expert_kernel, m, capacity),
+        functools.partial(expert_kernel, m, capacity, plan),
         out_shape=[
             jax.ShapeDtypeStruct(((m + 1) * capacity, width), F32),
             jax.ShapeDtypeStruct(((m + 1) * capacity, width), BF16),
         ],
-        in_specs=[in_vmem] * (2 * m + 3) + [pl.BlockSpec(memory_space=pl.ANY)] * 3,
+        in_specs=[in_vmem] * (2 * m + 3 + len(held)) + [in_hbm] * 3,
         out_specs=[in_vmem] * 2,
         scratch_shapes=[
             VMEM((total_rows, width), BF16),
-            VMEM((width, hid), BF16),
-            VMEM((width, hid), BF16),
-            VMEM((hid, width), BF16),
+            VMEM((step * fetched, hid), BF16),
+            VMEM((ring, wide, width), BF16),
             VMEM((2, total_rows, hid), F32),
             VMEM((total_rows, width), F32),
             VMEM((total_rows, hid), BF16),
-            pltpu.SemaphoreType.DMA((steps,)),
-            pltpu.SemaphoreType.DMA((steps,)),
+            pltpu.SemaphoreType.DMA((fetched,)),
             pltpu.SemaphoreType.DMA((parts,)),
         ],
-        compiler_params=pltpu.CompilerParams(vmem_limit_bytes=60 * MIB),
+        compiler_params=pltpu.CompilerParams(vmem_limit_bytes=(31 if roomy else 58) * MIB),
         cost_estimate=pl.CostEstimate(
             flops=2 * total_rows * 3 * width * hid, bytes_accessed=weight_bytes, transcendentals=0
         ),
         name="experts",
-    )(*mine, *theirs, share_mine, share_theirs, own, w_gate[0], w_up[0], w_down[0])
+    )(*mine, *theirs, share_mine, share_theirs, own, *held, gate_hbm, up_hbm, down_hbm)
 
     got = lax.ppermute(give, "tp", SWAP)
     *back, share_back, own_back = pl.pallas_call(
@@ -254,7 +358,7 @@
         out_shape=[block] * m + [half_block] * 2,
         in_specs=[in_vmem] * 2,
         out_specs=[in_vmem] * (m + 2),
-        compiler_params=pltpu.CompilerParams(vmem_limit_bytes=(12 if m < 8 else 40) * MIB),
+        compiler_params=pltpu.CompilerParams(vmem_limit_bytes=(8 if m < 8 else 40) * MIB),
         name="sum",
     )(keep, got)
 
@@ -266,7 +370,7 @@
         out_shape=jax.ShapeDtypeStruct((rows_here, half), BF16),
         in_specs=[in_vmem] * (2 * m + 4),
         out_specs=in_vmem,
-        compiler_params=pltpu.CompilerParams(vmem_limit_bytes=(12 if m < 8 else 40) * MIB),
+        compiler_params=pltpu.CompilerParams(vmem_limit_bytes=(8 if m < 8 else 40) * MIB),
         name="combine",
     )(routes_t, level_t, *mine, *theirs, share_back, own_back)
     return (context, moe_output)

time: 61.3 us -> 61.6 us (level)
  Pallas kernels: 23.7 us -> 30 us
  local copies, waits for them, and re-layouts: 3.84 us -> 0.01 us
  waiting for transfers between devices: 18.2 us -> 16.1 us
  starting transfers between devices: 13 us -> 14.6 us
  matrix products: 1.32 us -> 0 us
    ppermute x6, waiting for transfers between devices: 15.9 us -> 10.3 us  [body(): lax.ppermute(b, axes, route_of(count, pair))]
    pallas_call x1 -> x2, Pallas kernels: 22.1 us -> 27.6 us  [the longest x1 17 us: body(): pl.pallas_call(functools.partial(expert_kernel, m, capacity, plan), out_s...]
    unnamed x37 -> x4, local copies, waits for them, and re-layouts: 3.84 us -> 0.01 us
    ppermute x1, waiting for transfers between devices: 0.01 us -> 3.45 us  [body(): share_back = lax.ppermute(share_back, axes, route_of(count, (1, 1)))]
    dot_general x2 -> x0, matrix products: 1.32 us -> none  [the longest x1 0.81 us: attention(): jnp.einsum('rhd,rkd->rhk', query_heads, keys, preferred_element_type=jnp....]
    ppermute x6, starting transfers between devices: 10.2 us -> 11.3 us  [body(): lax.ppermute(b, axes, route_of(count, pair))]
    pallas_call x1, Pallas kernels: 0.46 us -> 1.32 us  [body(): pl.pallas_call(functools.partial(dispatch_kernel, pairs, span, capacity),...]
    ppermute x1, starting transfers between devices: 1.48 us -> 0.73 us  [body(): share_back = lax.ppermute(share_back, axes, route_of(count, (1, 1)))]
  transfers between devices with their start and end apart: 16 -> 16, of which waited for: 8 -> 5; matrix products, arithmetic and copies ran while one was open for 4% -> 0% of each run, Pallas kernels for 0% -> 17%
where the time goes in v2:
time: 61.6 us; the launch traced here: 61.5 us
  Pallas kernels  30 us (49%)
  waiting for transfers between devices  16.1 us (26%)
  starting transfers between devices  14.6 us (24%)
  between operations  0.75 us (1%)
    pallas_call x1, Pallas kernels, body(): pl.pallas_call(functools.partial(expert_kernel, m, capacity, plan), out_s...  17 us
    ppermute x6, starting transfers between devices, body(): lax.ppermute(b, axes, route_of(count, pair))  11.3 us
    pallas_call x1, Pallas kernels, body(): pl.pallas_call(functools.partial(attention_kernel, loads), out_shape=[jax...  10.6 us
    ppermute x6, waiting for transfers between devices, body(): lax.ppermute(b, axes, route_of(count, pair))  10.3 us
    ppermute x1, waiting for transfers between devices, body(): share_back = lax.ppermute(share_back, axes, route_of(count, (1, 1)))  3.45 us
    ppermute x1, waiting for transfers between devices, body(): got = lax.ppermute(give, 'tp', SWAP)  1.47 us
    pallas_call x1, Pallas kernels, body(): pl.pallas_call(functools.partial(dispatch_kernel, pairs, span, capacity),...  1.32 us
  transfers between devices with their start and end apart: 16, of which 5 were waited for; matrix products, arithmetic and copies ran while one was open for 0% of the time, Pallas kernels for 17%

profile of v2, /device:TPU:0, one launch (start us, length us, event | category | flops | bytes accessed | tf_op | source)
XLA Modules:
  0.0 61.5 jit_solution(9490541138490809028)
XLA Ops:
  0.6 1.3 %dispatch.1 = (bf16[8,7168]{1,0:T(8,128)(2,1)S(1)}, bf16[8,7168]{1,0:T(8,128)(2,1)S(1)}, bf16[8,7168]{1,0:T(8,128)(2,1)S(1)}, bf16[8,3584]{1,0:T(8,128)(2,1)S(1)}, bf16[8,7168]{1,0:T(8,128)(2,1)S(1)}) custom-call(s32[3,16]{1,0:T(4,128)} %bitcast.5, bf16[16,7168]{1,0:T(8,128)(2,1)} %x_hbm.1), custom_call_target="tpu_custom_call" | custom-call | tf_op jit(solution)/shard_map/dispatch/pallas_call | solution.py:264
  2.0 4.1 %collective-permute-start = (bf16[8,7168]{1,0:T(8,128)(2,1)S(1)}, bf16[8,7168]{1,0:T(8,128)(2,1)S(1)}, u32[]{:S(2)}, u32[]{:S(2)}) collective-permute-start(bf16[8,7168]{1,0:T(8,128)(2,1)S(1)} %get-tuple-element.36), channel_id=1, source_target_pairs={{0,8},{1,13},{2,10},{3,15},{4,12},{5,9},{6,14},{7,11},{8,0},{9,5},... | collective-permute-start | bytes 344072 | tf_op jit(solution)/shard_map/ppermute | solution.py:278
  6.1 1.3 %collective-permute-start.1 = (bf16[8,7168]{1,0:T(8,128)(2,1)S(1)}, bf16[8,7168]{1,0:T(8,128)(2,1)S(1)}, u32[]{:S(2)}, u32[]{:S(2)}) collective-permute-start(bf16[8,7168]{1,0:T(8,128)(2,1)S(1)} %get-tuple-element.37), channel_id=1, source_target_pairs={{0,10},{1,15},{2,8},{3,13},{4,14},{5,11},{6,12},{7,9},{8,2},{9,7},... | collective-permute-start | bytes 344072 | tf_op jit(solution)/shard_map/ppermute | solution.py:278
  7.3 1.6 %collective-permute-start.2 = (bf16[8,7168]{1,0:T(8,128)(2,1)S(1)}, bf16[8,7168]{1,0:T(8,128)(2,1)S(1)}, u32[]{:S(2)}, u32[]{:S(2)}) collective-permute-start(bf16[8,7168]{1,0:T(8,128)(2,1)S(1)} %get-tuple-element.38), channel_id=1, source_target_pairs={{0,4},{1,7},{2,6},{3,5},{4,0},{5,3},{6,2},{7,1},{8,12},{9,15},{10,... | collective-permute-start | bytes 344072 | tf_op jit(solution)/shard_map/ppermute | solution.py:278
  8.9 0.5 collective-permute-start.3
  9.4 10.6 %attention.1 = (bf16[4,8192]{1,0:T(4,128)(2,1)}, bf16[512,1280]{1,0:T(8,128)(2,1)S(1)}, bf16[512,1280]{1,0:T(8,128)(2,1)S(1)}, bf16[512,1280]{1,0:T(8,128)(2,1)S...) custom-call(s32[4]{0:T(128)} %refs_0_.1, ...), custom_call_target="tpu_custom_call" | custom-call | flops 134217728 | bytes 25165824 | tf_op jit(solution)/shard_map/attention/pallas_call | solution.py:296
  20.0 0.0 collective-permute-done.3.refs_6_
  20.0 0.0 collective-permute-done.refs_0_
  20.0 0.0 collective-permute-done.2.refs_2_
  20.0 0.1 collective-permute-start.4
  20.1 0.5 collective-permute-start.5
  20.6 0.1 collective-permute-start.6
  20.7 0.4 collective-permute-start.7
  21.1 0.9 %collective-permute-done.7.refs_7_ = bf16[8,3584]{1,0:T(8,128)(2,1)S(1)} collective-permute-done((bf16[8,3584]{1,0:T(8,128)(2,1)S(1)}, bf16[8,3584]{1,0:T(8,128)(2,1)S(1)}, u32[]{:S(2)}, u32[]{:S(2)}) %collective-permute-start.7) | collective-permute-done | bytes 57376 | tf_op jit(solution)/shard_map/ppermute | solution.py:323
  22.0 17.0 %experts.1 = (f32[32,7168]{1,0:T(8,128)S(1)}, bf16[32,7168]{1,0:T(8,128)(2,1)S(1)}) custom-call(bf16[8,7168]{1,0:T(8,128)(2,1)S(1)} %collective-permute-done.refs_0_, bf16[8,7168]{1,0:T(8,128)(2,1)S(1)} %collective-permute-done.1.refs_1_, bf16[8,7168]{1,0:T(8,128)(2,1)S(1)} %collective-permute-done.2.refs_2_, ...), custom_call_target="tpu_custom_call" | custom-call | flops 3523215360 | bytes 34078720 | tf_op jit(solution)/shard_map/experts/pallas_call | solution.py:330
  39.1 0.0 copy-start
  39.1 0.0 copy-start.1
  39.1 0.4 collective-permute-start.8
  39.5 1.5 %collective-permute-done.8.got = bf16[32,7168]{1,0:T(8,128)(2,1)S(1)} collective-permute-done((bf16[32,7168]{1,0:T(8,128)(2,1)S(1)}, bf16[32,7168]{1,0:T(8,128)(2,1)S(1)}, u32[]{:S(2)}, u32[]{:S(2)}) %collective-permute-start.8) | collective-permute-done | bytes 458784 | tf_op jit(solution)/shard_map/ppermute | solution.py:355
  41.0 0.1 sum.1
  41.0 3.0 %collective-permute-start.9 = (bf16[8,7168]{1,0:T(8,128)(2,1)S(1)}, bf16[8,7168]{1,0:T(8,128)(2,1)S(1)}, u32[]{:S(2)}, u32[]{:S(2)}) collective-permute-start(bf16[8,7168]{1,0:T(8,128)(2,1)S(1)} %get-tuple-element.65), channel_id=1, source_target_pairs={{0,8},{1,13},{2,10},{3,15},{4,12},{5,9},{6,14},{7,11},{8,0},{9,5},... | collective-permute-start | bytes 344072 | tf_op jit(solution)/shard_map/ppermute | solution.py:365
  44.1 0.9 %collective-permute-start.10 = (bf16[8,7168]{1,0:T(8,128)(2,1)S(1)}, bf16[8,7168]{1,0:T(8,128)(2,1)S(1)}, u32[]{:S(2)}, u32[]{:S(2)}) collective-permute-start(bf16[8,7168]{1,0:T(8,128)(2,1)S(1)} %get-tuple-element.66), channel_id=1, source_target_pairs={{0,10},{1,15},{2,8},{3,13},{4,14},{5,11},{6,12},{7,9},{8,2},{9,7},... | collective-permute-start | bytes 344072 | tf_op jit(solution)/shard_map/ppermute | solution.py:365
  45.0 0.4 collective-permute-start.11
  45.4 7.5 %collective-permute-done.9.refs_0_ = bf16[8,7168]{1,0:T(8,128)(2,1)S(1)} collective-permute-done((bf16[8,7168]{1,0:T(8,128)(2,1)S(1)}, bf16[8,7168]{1,0:T(8,128)(2,1)S(1)}, u32[]{:S(2)}, u32[]{:S(2)}) %collective-permute-start.9) | collective-permute-done | bytes 114720 | tf_op jit(solution)/shard_map/ppermute | solution.py:365
  52.9 0.0 collective-permute-start.12
  52.9 2.7 %collective-permute-done.10.refs_1_ = bf16[8,7168]{1,0:T(8,128)(2,1)S(1)} collective-permute-done((bf16[8,7168]{1,0:T(8,128)(2,1)S(1)}, bf16[8,7168]{1,0:T(8,128)(2,1)S(1)}, u32[]{:S(2)}, u32[]{:S(2)}) %collective-permute-start.10) | collective-permute-done | bytes 114720 | tf_op jit(solution)/shard_map/ppermute | solution.py:365
  55.7 0.5 collective-permute-start.14
  56.2 0.7 %collective-permute-start.15 = (bf16[8,3584]{1,0:T(8,128)(2,1)S(1)}, bf16[8,3584]{1,0:T(8,128)(2,1)S(1)}, u32[]{:S(2)}, u32[]{:S(2)}) collective-permute-start(bf16[8,3584]{1,0:T(8,128)(2,1)S(1)} %get-tuple-element.68), channel_id=1, source_target_pairs={{0,2},{1,3},{2,0},{3,1},{4,6},{5,7},{6,4},{7,5},{8,10},{9,11},{10,... | collective-permute-start | bytes 172040 | tf_op jit(solution)/shard_map/ppermute | solution.py:366
  56.9 3.4 %collective-permute-done.15.refs_6_ = bf16[8,3584]{1,0:T(8,128)(2,1)S(1)} collective-permute-done((bf16[8,3584]{1,0:T(8,128)(2,1)S(1)}, bf16[8,3584]{1,0:T(8,128)(2,1)S(1)}, u32[]{:S(2)}, u32[]{:S(2)}) %collective-permute-start.15) | collective-permute-done | bytes 57376 | tf_op jit(solution)/shard_map/ppermute | solution.py:366
  60.4 0.0 collective-permute-done.13.refs_4_
  60.4 0.0 collective-permute-done.14.refs_5_
  60.4 1.1 %combine.1 = bf16[16,3584]{1,0:T(8,128)(2,1)} custom-call(s32[3,16]{1,0:T(4,128)S(1)} %bitcast.6, s32[3,16]{1,0:T(4,128)S(1)} %bitcast.7, bf16[8,7168]{1,0:T(8,128)(2,1)S(1)} %collective-permute-done.9.refs_0_, bf16[8,7168]{1,0:T(8,128)(2,1)S(1)} %collective-permute-done.10.refs_1_, bf16[8,7168]{1,0:T(8,128)(2,1)S(1)} %collective-permute-done.11.refs_2_, ...), custom_call_target="tpu_custom_call" | custom-call | tf_op jit(solution)/shard_map/combine/pallas_call | solution.py:368
  (9 shorter events, 0.0 us)
Async XLA Ops:
  2.0 18.1 %collective-permute-start = (bf16[8,7168]{1,0:T(8,128)(2,1)S(1)}, bf16[8,7168]{1,0:T(8,128)(2,1)S(1)}, u32[]{:S(2)}, u32[]{:S(2)}) collective-permute-start(bf16[8,7168]{1,0:T(8,128)(2,1)S(1)} %get-tuple-element.36), channel_id=1, source_target_pairs={{0,8},{1,13},{2,10},{3,15},{4,12},{5,9},{6,14},{7,11},{8,0},{9,5},... | collective-permute-start | bytes 344072 | tf_op jit(solution)/shard_map/ppermute | solution.py:278
  6.1 14.0 %collective-permute-start.1 = (bf16[8,7168]{1,0:T(8,128)(2,1)S(1)}, bf16[8,7168]{1,0:T(8,128)(2,1)S(1)}, u32[]{:S(2)}, u32[]{:S(2)}) collective-permute-start(bf16[8,7168]{1,0:T(8,128)(2,1)S(1)} %get-tuple-element.37), channel_id=1, source_target_pairs={{0,10},{1,15},{2,8},{3,13},{4,14},{5,11},{6,12},{7,9},{8,2},{9,7},... | collective-permute-start | bytes 344072 | tf_op jit(solution)/shard_map/ppermute | solution.py:278
  7.3 12.7 %collective-permute-start.2 = (bf16[8,7168]{1,0:T(8,128)(2,1)S(1)}, bf16[8,7168]{1,0:T(8,128)(2,1)S(1)}, u32[]{:S(2)}, u32[]{:S(2)}) collective-permute-start(bf16[8,7168]{1,0:T(8,128)(2,1)S(1)} %get-tuple-element.38), channel_id=1, source_target_pairs={{0,4},{1,7},{2,6},{3,5},{4,0},{5,3},{6,2},{7,1},{8,12},{9,15},{10,... | collective-permute-start | bytes 344072 | tf_op jit(solution)/shard_map/ppermute | solution.py:278
  8.9 11.1 %collective-permute-start.3 = (bf16[8,3584]{1,0:T(8,128)(2,1)S(1)}, bf16[8,3584]{1,0:T(8,128)(2,1)S(1)}, u32[]{:S(2)}, u32[]{:S(2)}) collective-permute-start(bf16[8,3584]{1,0:T(8,128)(2,1)S(1)} %get-tuple-element.39), channel_id=1, source_target_pairs={{0,2},{1,3},{2,0},{3,1},{4,6},{5,7},{6,4},{7,5},{8,10},{9,11},{10,... | collective-permute-start | bytes 172040 | tf_op jit(solution)/shard_map/ppermute | solution.py:279
  20.0 2.0 %collective-permute-start.4 = (bf16[8,7168]{1,0:T(8,128)(2,1)S(1)}, bf16[8,7168]{1,0:T(8,128)(2,1)S(1)}, u32[]{:S(2)}, u32[]{:S(2)}) collective-permute-start(bf16[8,7168]{1,0:T(8,128)(2,1)S(1)} %collective-permute-done.refs_0_), channel_id=1, source_target_pairs={{0,1},{1,0},{2,3},{3,2},{4,5},{5,4},{6,7},{7,6},{8,9},{9,8},{10,11... | collective-permute-start | bytes 344072 | tf_op jit(solution)/shard_map/ppermute | solution.py:322
  20.1 1.9 %collective-permute-start.5 = (bf16[8,7168]{1,0:T(8,128)(2,1)S(1)}, bf16[8,7168]{1,0:T(8,128)(2,1)S(1)}, u32[]{:S(2)}, u32[]{:S(2)}) collective-permute-start(bf16[8,7168]{1,0:T(8,128)(2,1)S(1)} %collective-permute-done.1.refs_1_), channel_id=1, source_target_pairs={{0,1},{1,0},{2,3},{3,2},{4,5},{5,4},{6,7},{7,6},{8,9},{9,8},{10,11... | collective-permute-start | bytes 344072 | tf_op jit(solution)/shard_map/ppermute | solution.py:322
  20.6 1.4 %collective-permute-start.6 = (bf16[8,7168]{1,0:T(8,128)(2,1)S(1)}, bf16[8,7168]{1,0:T(8,128)(2,1)S(1)}, u32[]{:S(2)}, u32[]{:S(2)}) collective-permute-start(bf16[8,7168]{1,0:T(8,128)(2,1)S(1)} %collective-permute-done.2.refs_2_), channel_id=1, source_target_pairs={{0,1},{1,0},{2,3},{3,2},{4,5},{5,4},{6,7},{7,6},{8,9},{9,8},{10,11... | collective-permute-start | bytes 344072 | tf_op jit(solution)/shard_map/ppermute | solution.py:322
  20.7 1.3 %collective-permute-start.7 = (bf16[8,3584]{1,0:T(8,128)(2,1)S(1)}, bf16[8,3584]{1,0:T(8,128)(2,1)S(1)}, u32[]{:S(2)}, u32[]{:S(2)}) collective-permute-start(bf16[8,3584]{1,0:T(8,128)(2,1)S(1)} %collective-permute-done.3.refs_6_), channel_id=1, source_target_pairs={{0,1},{1,0},{2,3},{3,2},{4,5},{5,4},{6,7},{7,6},{8,9},{9,8},{10,11... | collective-permute-start | bytes 172040 | tf_op jit(solution)/shard_map/ppermute | solution.py:323
  39.1 21.3 %copy-start = (s32[16,3]{0,1:T(4,128)S(1)}, s32[16,3]{0,1:T(4,128)}, u32[]{:S(2)}) copy-start(s32[16,3]{0,1:T(4,128)} %param.15) | copy-start | bytes 580
  39.1 21.3 %copy-start.1 = (s32[16,3]{0,1:T(4,128)S(1)}, s32[16,3]{0,1:T(4,128)}, u32[]{:S(2)}) copy-start(s32[16,3]{0,1:T(4,128)} %param.16) | copy-start | bytes 580
  39.1 1.9 %collective-permute-start.8 = (bf16[32,7168]{1,0:T(8,128)(2,1)S(1)}, bf16[32,7168]{1,0:T(8,128)(2,1)S(1)}, u32[]{:S(2)}, u32[]{:S(2)}) collective-permute-start(bf16[32,7168]{1,0:T(8,128)(2,1)S(1)} %get-tuple-element.64), channel_id=1, source_target_pairs={{0,1},{1,0},{2,3},{3,2},{4,5},{5,4},{6,7},{7,6},{8,9},{9,8},{10,11... | collective-permute-start | bytes 1376264 | tf_op jit(solution)/shard_map/ppermute | solution.py:355
  41.0 11.9 %collective-permute-start.9 = (bf16[8,7168]{1,0:T(8,128)(2,1)S(1)}, bf16[8,7168]{1,0:T(8,128)(2,1)S(1)}, u32[]{:S(2)}, u32[]{:S(2)}) collective-permute-start(bf16[8,7168]{1,0:T(8,128)(2,1)S(1)} %get-tuple-element.65), channel_id=1, source_target_pairs={{0,8},{1,13},{2,10},{3,15},{4,12},{5,9},{6,14},{7,11},{8,0},{9,5},... | collective-permute-start | bytes 344072 | tf_op jit(solution)/shard_map/ppermute | solution.py:365
  44.1 11.6 %collective-permute-start.10 = (bf16[8,7168]{1,0:T(8,128)(2,1)S(1)}, bf16[8,7168]{1,0:T(8,128)(2,1)S(1)}, u32[]{:S(2)}, u32[]{:S(2)}) collective-permute-start(bf16[8,7168]{1,0:T(8,128)(2,1)S(1)} %get-tuple-element.66), channel_id=1, source_target_pairs={{0,10},{1,15},{2,8},{3,13},{4,14},{5,11},{6,12},{7,9},{8,2},{9,7},... | collective-permute-start | bytes 344072 | tf_op jit(solution)/shard_map/ppermute | solution.py:365
  45.0 10.7 %collective-permute-start.11 = (bf16[8,7168]{1,0:T(8,128)(2,1)S(1)}, bf16[8,7168]{1,0:T(8,128)(2,1)S(1)}, u32[]{:S(2)}, u32[]{:S(2)}) collective-permute-start(bf16[8,7168]{1,0:T(8,128)(2,1)S(1)} %get-tuple-element.67), channel_id=1, source_target_pairs={{0,4},{1,7},{2,6},{3,5},{4,0},{5,3},{6,2},{7,1},{8,12},{9,15},{10,... | collective-permute-start | bytes 344072 | tf_op jit(solution)/shard_map/ppermute | solution.py:365
  52.9 7.4 %collective-permute-start.12 = (bf16[8,7168]{1,0:T(8,128)(2,1)S(1)}, bf16[8,7168]{1,0:T(8,128)(2,1)S(1)}, u32[]{:S(2)}, u32[]{:S(2)}) collective-permute-start(bf16[8,7168]{1,0:T(8,128)(2,1)S(1)} %collective-permute-done.9.refs_0_), channel_id=1, source_target_pairs={{0,1},{1,0},{2,3},{3,2},{4,5},{5,4},{6,7},{7,6},{8,9},{9,8},{10,11... | collective-permute-start | bytes 344072 | tf_op jit(solution)/shard_map/ppermute | solution.py:367
  55.7 4.7 %collective-permute-start.13 = (bf16[8,7168]{1,0:T(8,128)(2,1)S(1)}, bf16[8,7168]{1,0:T(8,128)(2,1)S(1)}, u32[]{:S(2)}, u32[]{:S(2)}) collective-permute-start(bf16[8,7168]{1,0:T(8,128)(2,1)S(1)} %collective-permute-done.10.refs_1_), channel_id=1, source_target_pairs={{0,1},{1,0},{2,3},{3,2},{4,5},{5,4},{6,7},{7,6},{8,9},{9,8},{10,11... | collective-permute-start | bytes 344072 | tf_op jit(solution)/shard_map/ppermute | solution.py:367
  55.7 4.7 %collective-permute-start.14 = (bf16[8,7168]{1,0:T(8,128)(2,1)S(1)}, bf16[8,7168]{1,0:T(8,128)(2,1)S(1)}, u32[]{:S(2)}, u32[]{:S(2)}) collective-permute-start(bf16[8,7168]{1,0:T(8,128)(2,1)S(1)} %collective-permute-done.11.refs_2_), channel_id=1, source_target_pairs={{0,1},{1,0},{2,3},{3,2},{4,5},{5,4},{6,7},{7,6},{8,9},{9,8},{10,11... | collective-permute-start | bytes 344072 | tf_op jit(solution)/shard_map/ppermute | solution.py:367
  56.2 4.2 %collective-permute-start.15 = (bf16[8,3584]{1,0:T(8,128)(2,1)S(1)}, bf16[8,3584]{1,0:T(8,128)(2,1)S(1)}, u32[]{:S(2)}, u32[]{:S(2)}) collective-permute-start(bf16[8,3584]{1,0:T(8,128)(2,1)S(1)} %get-tuple-element.68), channel_id=1, source_target_pairs={{0,2},{1,3},{2,0},{3,1},{4,6},{5,7},{6,4},{7,5},{8,10},{9,11},{10,... | collective-permute-start | bytes 172040 | tf_op jit(solution)/shard_map/ppermute | solution.py:366

commit v3 on v2

--- a/solution.py
+++ b/solution.py
@@ -12,6 +12,7 @@
 TOP = 3
 MIB = 2**20
 HEAD = 1024
+AHEAD = 4
 SWAP = [(0, 1), (1, 0)]
 VMEM = pltpu.VMEM
 BF16 = jnp.bfloat16
@@ -48,8 +49,9 @@
         copy = pltpu.make_async_copy(
             weights[which].at[pl.ds(start, rows)], held[i], sems.at[i]
         )
+        copies.append(copy)
+    for copy in copies[:AHEAD]:
         copy.start()
-        copies.append(copy)
     requests, slots, size = k_ref.shape
     heads = q_ref.shape[1] // size
     planes = packed.shape[0]
@@ -62,6 +64,8 @@
         )
     own[2].wait()
     own[3].wait()
+    for copy in copies[AHEAD:]:
+        copy.start()
     for r in range(requests):
         every = pl.ds(r, heads, stride=requests)
         query = jnp.concatenate([packed[j, every, :] for j in range(planes)], axis=1).astype(BF16)
@@ -154,8 +158,9 @@
     parts = width // wide
 
     fetches, place = {}, 0
-    for j, (ranges, source) in enumerate(zip(plan, (gate_hbm, up_hbm))):
-        for start, rows, i in ranges:
+    for ranges in zip(*plan):
+        for j, (start, rows, i) in enumerate(ranges):
+            source = (gate_hbm, up_hbm)[j]
             if i < 0:
                 fetches[j, start] = (
                     place,
@@ -166,16 +171,20 @@
                     ),
                 )
                 place += rows
-    for _, copy in fetches.values():
-        copy.start()
 
     def fetch(i):
         return pltpu.make_async_copy(
             down_hbm.at[pl.ds(i * wide, wide)], down_w.at[i % ring], down_sem.at[i]
         )
 
-    for i in range(min(ring, parts)):
-        fetch(i).start()
+    queue = [copy for _, copy in fetches.values()] + [fetch(i) for i in range(min(ring, parts))]
+
+    def ask(number):
+        for copy in queue[:number]:
+            copy.start()
+        del queue[:number]
+
+    ask(AHEAD)
     two = 2 * capacity
     for i in range(m):
         x[i * two : (i + 1) * two, :] = jnp.concatenate(
@@ -184,16 +193,18 @@
     for c, part in ((core, share_mine), (1 - core, share_theirs)):
         at = pl.ds(pl.multiple_of(c * half, 128), half)
         x[m * two : (m + 1) * two, at] = jnp.concatenate([part[...], own[:, at]], axis=0)
-    for j, ranges in enumerate(plan):
-        for start, rows, i in ranges:
+    for ranges in zip(*plan):
+        for j, (start, rows, i) in enumerate(ranges):
             if i < 0:
                 place, copy = fetches[j, start]
                 copy.wait()
+                ask(1)
                 weight = rest_w[place : place + rows, :]
             else:
                 weight = parts_held[i][...]
             term = jnp.dot(x[:, start : start + rows], weight, preferred_element_type=F32)
             total[j] = term if start == 0 else total[j] + term
+    ask(len(queue))
     gate = total[0]
     hidden[...] = (gate / (1.0 + jnp.exp(-gate)) * total[1]).astype(BF16)
     for i in range(parts):
@@ -364,6 +375,7 @@
 
     mine = [lax.ppermute(b, axes, route_of(count, pair)) for b, pair in zip(back, pairs)]
     share_back = lax.ppermute(share_back, axes, route_of(count, (1, 1)))
+    *mine, share_back = lax.optimization_barrier((*mine, share_back))
     theirs = [lax.ppermute(b, "tp", SWAP) for b in mine]
     moe_output = pl.pallas_call(
         functools.partial(combine_kernel, pairs, span, capacity),

time: 61.6 us -> 54.6 us (0.89)
  Pallas kernels: 30 us -> 25.9 us
  waiting for transfers between devices: 16.1 us -> 12.9 us
    ppermute x6, waiting for transfers between devices: 10.3 us -> 4.38 us  [body(): lax.ppermute(b, axes, route_of(count, pair))]
    pallas_call x1, Pallas kernels: 17 us -> 13.3 us  [body(): pl.pallas_call(functools.partial(expert_kernel, m, capacity, plan), out_s...]
    ppermute x1, waiting for transfers between devices: 3.45 us -> 4.83 us  [body(): share_back = lax.ppermute(share_back, axes, route_of(count, (1, 1)))]
    ppermute x6, waiting for transfers between devices: 0.02 us -> 1.33 us  [body(): theirs = [lax.ppermute(b, 'tp', SWAP) for b in mine]]
  transfers between devices with their start and end apart: 16 -> 16, of which waited for: 5 -> 8; matrix products, arithmetic and copies ran while one was open for 0% -> 0% of each run, Pallas kernels for 17% -> 19%
where the time goes in v3:
time: 54.6 us; the launch traced here: 54.4 us
  Pallas kernels  25.9 us (47%)
  starting transfers between devices  14.9 us (27%)
  waiting for transfers between devices  12.9 us (24%)
  between operations  0.73 us (1%)
    pallas_call x1, Pallas kernels, body(): pl.pallas_call(functools.partial(expert_kernel, m, capacity, plan), out_s...  13.3 us
    ppermute x6, starting transfers between devices, body(): lax.ppermute(b, axes, route_of(count, pair))  11.3 us
    pallas_call x1, Pallas kernels, body(): pl.pallas_call(functools.partial(attention_kernel, loads), out_shape=[jax...  10.1 us
    ppermute x1, waiting for transfers between devices, body(): share_back = lax.ppermute(share_back, axes, route_of(count, (1, 1)))  4.83 us
    ppermute x6, waiting for transfers between devices, body(): lax.ppermute(b, axes, route_of(count, pair))  4.38 us
    ppermute x1, waiting for transfers between devices, body(): got = lax.ppermute(give, 'tp', SWAP)  1.46 us
    ppermute x6, waiting for transfers between devices, body(): theirs = [lax.ppermute(b, 'tp', SWAP) for b in mine]  1.33 us
    pallas_call x1, Pallas kernels, body(): pl.pallas_call(functools.partial(dispatch_kernel, pairs, span, capacity),...  1.32 us
  transfers between devices with their start and end apart: 16, of which 8 were waited for; matrix products, arithmetic and copies ran while one was open for 0% of the time, Pallas kernels for 19%

profile of v3, /device:TPU:0, one launch (start us, length us, event | category | flops | bytes accessed | tf_op | source)
XLA Modules:
  0.0 54.4 jit_solution(17423824117801222904)
XLA Ops:
  0.6 1.3 %dispatch.1 = (bf16[8,7168]{1,0:T(8,128)(2,1)S(1)}, bf16[8,7168]{1,0:T(8,128)(2,1)S(1)}, bf16[8,7168]{1,0:T(8,128)(2,1)S(1)}, bf16[8,3584]{1,0:T(8,128)(2,1)S(1)}, bf16[8,7168]{1,0:T(8,128)(2,1)S(1)}) custom-call(s32[3,16]{1,0:T(4,128)} %bitcast.5, bf16[16,7168]{1,0:T(8,128)(2,1)} %x_hbm.1), custom_call_target="tpu_custom_call" | custom-call | tf_op jit(solution)/shard_map/dispatch/pallas_call | solution.py:275
  2.0 4.1 %collective-permute-start = (bf16[8,7168]{1,0:T(8,128)(2,1)S(1)}, bf16[8,7168]{1,0:T(8,128)(2,1)S(1)}, u32[]{:S(2)}, u32[]{:S(2)}) collective-permute-start(bf16[8,7168]{1,0:T(8,128)(2,1)S(1)} %get-tuple-element.40), channel_id=1, source_target_pairs={{0,8},{1,13},{2,10},{3,15},{4,12},{5,9},{6,14},{7,11},{8,0},{9,5},... | collective-permute-start | bytes 344072 | tf_op jit(solution)/shard_map/ppermute | solution.py:289
  6.1 1.3 %collective-permute-start.1 = (bf16[8,7168]{1,0:T(8,128)(2,1)S(1)}, bf16[8,7168]{1,0:T(8,128)(2,1)S(1)}, u32[]{:S(2)}, u32[]{:S(2)}) collective-permute-start(bf16[8,7168]{1,0:T(8,128)(2,1)S(1)} %get-tuple-element.41), channel_id=1, source_target_pairs={{0,10},{1,15},{2,8},{3,13},{4,14},{5,11},{6,12},{7,9},{8,2},{9,7},... | collective-permute-start | bytes 344072 | tf_op jit(solution)/shard_map/ppermute | solution.py:289
  7.3 1.6 %collective-permute-start.2 = (bf16[8,7168]{1,0:T(8,128)(2,1)S(1)}, bf16[8,7168]{1,0:T(8,128)(2,1)S(1)}, u32[]{:S(2)}, u32[]{:S(2)}) collective-permute-start(bf16[8,7168]{1,0:T(8,128)(2,1)S(1)} %get-tuple-element.42), channel_id=1, source_target_pairs={{0,4},{1,7},{2,6},{3,5},{4,0},{5,3},{6,2},{7,1},{8,12},{9,15},{10,... | collective-permute-start | bytes 344072 | tf_op jit(solution)/shard_map/ppermute | solution.py:289
  8.9 0.5 collective-permute-start.3
  9.4 10.1 %attention.1 = (bf16[4,8192]{1,0:T(4,128)(2,1)}, bf16[512,1280]{1,0:T(8,128)(2,1)S(1)}, bf16[512,1280]{1,0:T(8,128)(2,1)S(1)}, bf16[512,1280]{1,0:T(8,128)(2,1)S...) custom-call(s32[4]{0:T(128)} %refs_0_.1, ...), custom_call_target="tpu_custom_call" | custom-call | flops 134217728 | bytes 25165824 | tf_op jit(solution)/shard_map/attention/pallas_call | solution.py:307
  19.6 0.0 collective-permute-done.3.refs_6_
  19.6 0.0 collective-permute-done.1.refs_1_
  19.6 0.1 collective-permute-start.4
  19.7 0.5 collective-permute-start.5
  20.2 0.1 collective-permute-start.6
  20.3 0.4 collective-permute-start.7
  20.7 0.9 %collective-permute-done.7.refs_7_ = bf16[8,3584]{1,0:T(8,128)(2,1)S(1)} collective-permute-done((bf16[8,3584]{1,0:T(8,128)(2,1)S(1)}, bf16[8,3584]{1,0:T(8,128)(2,1)S(1)}, u32[]{:S(2)}, u32[]{:S(2)}) %collective-permute-start.7) | collective-permute-done | bytes 57376 | tf_op jit(solution)/shard_map/ppermute | solution.py:334
  21.6 13.3 %experts.1 = (f32[32,7168]{1,0:T(8,128)S(1)}, bf16[32,7168]{1,0:T(8,128)(2,1)S(1)}) custom-call(bf16[8,7168]{1,0:T(8,128)(2,1)S(1)} %collective-permute-done.refs_0_, bf16[8,7168]{1,0:T(8,128)(2,1)S(1)} %collective-permute-done.1.refs_1_, bf16[8,7168]{1,0:T(8,128)(2,1)S(1)} %collective-permute-done.2.refs_2_, ...), custom_call_target="tpu_custom_call" | custom-call | flops 3523215360 | bytes 34078720 | tf_op jit(solution)/shard_map/experts/pallas_call | solution.py:341
  34.9 0.0 copy-start
  34.9 0.0 copy-start.1
  34.9 0.4 collective-permute-start.8
  35.4 1.5 %collective-permute-done.8.got = bf16[32,7168]{1,0:T(8,128)(2,1)S(1)} collective-permute-done((bf16[32,7168]{1,0:T(8,128)(2,1)S(1)}, bf16[32,7168]{1,0:T(8,128)(2,1)S(1)}, u32[]{:S(2)}, u32[]{:S(2)}) %collective-permute-start.8) | collective-permute-done | bytes 458784 | tf_op jit(solution)/shard_map/ppermute | solution.py:366
  36.8 0.1 sum.1
  36.9 3.0 %collective-permute-start.9 = (bf16[8,7168]{1,0:T(8,128)(2,1)S(1)}, bf16[8,7168]{1,0:T(8,128)(2,1)S(1)}, u32[]{:S(2)}, u32[]{:S(2)}) collective-permute-start(bf16[8,7168]{1,0:T(8,128)(2,1)S(1)} %get-tuple-element.69), channel_id=1, source_target_pairs={{0,8},{1,13},{2,10},{3,15},{4,12},{5,9},{6,14},{7,11},{8,0},{9,5},... | collective-permute-start | bytes 344072 | tf_op jit(solution)/shard_map/ppermute | solution.py:376
  39.9 0.9 %collective-permute-start.10 = (bf16[8,7168]{1,0:T(8,128)(2,1)S(1)}, bf16[8,7168]{1,0:T(8,128)(2,1)S(1)}, u32[]{:S(2)}, u32[]{:S(2)}) collective-permute-start(bf16[8,7168]{1,0:T(8,128)(2,1)S(1)} %get-tuple-element.70), channel_id=1, source_target_pairs={{0,10},{1,15},{2,8},{3,13},{4,14},{5,11},{6,12},{7,9},{8,2},{9,7},... | collective-permute-start | bytes 344072 | tf_op jit(solution)/shard_map/ppermute | solution.py:376
  40.8 0.4 collective-permute-start.11
  41.3 1.1 %collective-permute-start.12 = (bf16[8,3584]{1,0:T(8,128)(2,1)S(1)}, bf16[8,3584]{1,0:T(8,128)(2,1)S(1)}, u32[]{:S(2)}, u32[]{:S(2)}) collective-permute-start(bf16[8,3584]{1,0:T(8,128)(2,1)S(1)} %get-tuple-element.72), channel_id=1, source_target_pairs={{0,2},{1,3},{2,0},{3,1},{4,6},{5,7},{6,4},{7,5},{8,10},{9,11},{10,... | collective-permute-start | bytes 172040 | tf_op jit(solution)/shard_map/ppermute | solution.py:377
  42.3 4.8 %collective-permute-done.12.refs_6_ = bf16[8,3584]{1,0:T(8,128)(2,1)S(1)} collective-permute-done((bf16[8,3584]{1,0:T(8,128)(2,1)S(1)}, bf16[8,3584]{1,0:T(8,128)(2,1)S(1)}, u32[]{:S(2)}, u32[]{:S(2)}) %collective-permute-start.12) | collective-permute-done | bytes 57376 | tf_op jit(solution)/shard_map/ppermute | solution.py:377
  47.2 1.6 %collective-permute-done.9.refs_0_ = bf16[8,7168]{1,0:T(8,128)(2,1)S(1)} collective-permute-done((bf16[8,7168]{1,0:T(8,128)(2,1)S(1)}, bf16[8,7168]{1,0:T(8,128)(2,1)S(1)}, u32[]{:S(2)}, u32[]{:S(2)}) %collective-permute-start.9) | collective-permute-done | bytes 114720 | tf_op jit(solution)/shard_map/ppermute | solution.py:376
  48.8 2.7 %collective-permute-done.10.refs_1_ = bf16[8,7168]{1,0:T(8,128)(2,1)S(1)} collective-permute-done((bf16[8,7168]{1,0:T(8,128)(2,1)S(1)}, bf16[8,7168]{1,0:T(8,128)(2,1)S(1)}, u32[]{:S(2)}, u32[]{:S(2)}) %collective-permute-start.10) | collective-permute-done | bytes 114720 | tf_op jit(solution)/shard_map/ppermute | solution.py:376
  51.5 0.5 collective-permute-start.14
  52.0 0.0 collective-permute-start.15
  52.0 0.8 %collective-permute-done.13.refs_3_ = bf16[8,7168]{1,0:T(8,128)(2,1)S(1)} collective-permute-done((bf16[8,7168]{1,0:T(8,128)(2,1)S(1)}, bf16[8,7168]{1,0:T(8,128)(2,1)S(1)}, u32[]{:S(2)}, u32[]{:S(2)}) %collective-permute-start.13) | collective-permute-done | bytes 114720 | tf_op jit(solution)/shard_map/ppermute | solution.py:379
  52.9 0.2 collective-permute-done.14.refs_4_
  53.0 0.3 collective-permute-done.15.refs_5_
  53.4 1.1 %combine.1 = bf16[16,3584]{1,0:T(8,128)(2,1)} custom-call(s32[3,16]{1,0:T(4,128)S(1)} %bitcast.6, s32[3,16]{1,0:T(4,128)S(1)} %bitcast.7, bf16[8,7168]{1,0:T(8,128)(2,1)S(1)} %collective-permute-done.9.refs_0_, bf16[8,7168]{1,0:T(8,128)(2,1)S(1)} %collective-permute-done.10.refs_1_, bf16[8,7168]{1,0:T(8,128)(2,1)S(1)} %collective-permute-done.11.refs_2_, ...), custom_call_target="tpu_custom_call" | custom-call | tf_op jit(solution)/shard_map/combine/pallas_call | solution.py:380
  (9 shorter events, 0.0 us)
Async XLA Ops:
  2.0 17.6 %collective-permute-start = (bf16[8,7168]{1,0:T(8,128)(2,1)S(1)}, bf16[8,7168]{1,0:T(8,128)(2,1)S(1)}, u32[]{:S(2)}, u32[]{:S(2)}) collective-permute-start(bf16[8,7168]{1,0:T(8,128)(2,1)S(1)} %get-tuple-element.40), channel_id=1, source_target_pairs={{0,8},{1,13},{2,10},{3,15},{4,12},{5,9},{6,14},{7,11},{8,0},{9,5},... | collective-permute-start | bytes 344072 | tf_op jit(solution)/shard_map/ppermute | solution.py:289
  6.1 13.5 %collective-permute-start.1 = (bf16[8,7168]{1,0:T(8,128)(2,1)S(1)}, bf16[8,7168]{1,0:T(8,128)(2,1)S(1)}, u32[]{:S(2)}, u32[]{:S(2)}) collective-permute-start(bf16[8,7168]{1,0:T(8,128)(2,1)S(1)} %get-tuple-element.41), channel_id=1, source_target_pairs={{0,10},{1,15},{2,8},{3,13},{4,14},{5,11},{6,12},{7,9},{8,2},{9,7},... | collective-permute-start | bytes 344072 | tf_op jit(solution)/shard_map/ppermute | solution.py:289
  7.3 12.3 %collective-permute-start.2 = (bf16[8,7168]{1,0:T(8,128)(2,1)S(1)}, bf16[8,7168]{1,0:T(8,128)(2,1)S(1)}, u32[]{:S(2)}, u32[]{:S(2)}) collective-permute-start(bf16[8,7168]{1,0:T(8,128)(2,1)S(1)} %get-tuple-element.42), channel_id=1, source_target_pairs={{0,4},{1,7},{2,6},{3,5},{4,0},{5,3},{6,2},{7,1},{8,12},{9,15},{10,... | collective-permute-start | bytes 344072 | tf_op jit(solution)/shard_map/ppermute | solution.py:289
  8.9 10.7 %collective-permute-start.3 = (bf16[8,3584]{1,0:T(8,128)(2,1)S(1)}, bf16[8,3584]{1,0:T(8,128)(2,1)S(1)}, u32[]{:S(2)}, u32[]{:S(2)}) collective-permute-start(bf16[8,3584]{1,0:T(8,128)(2,1)S(1)} %get-tuple-element.43), channel_id=1, source_target_pairs={{0,2},{1,3},{2,0},{3,1},{4,6},{5,7},{6,4},{7,5},{8,10},{9,11},{10,... | collective-permute-start | bytes 172040 | tf_op jit(solution)/shard_map/ppermute | solution.py:290
  19.6 2.0 %collective-permute-start.4 = (bf16[8,7168]{1,0:T(8,128)(2,1)S(1)}, bf16[8,7168]{1,0:T(8,128)(2,1)S(1)}, u32[]{:S(2)}, u32[]{:S(2)}) collective-permute-start(bf16[8,7168]{1,0:T(8,128)(2,1)S(1)} %collective-permute-done.refs_0_), channel_id=1, source_target_pairs={{0,1},{1,0},{2,3},{3,2},{4,5},{5,4},{6,7},{7,6},{8,9},{9,8},{10,11... | collective-permute-start | bytes 344072 | tf_op jit(solution)/shard_map/ppermute | solution.py:333
  19.7 1.9 %collective-permute-start.5 = (bf16[8,7168]{1,0:T(8,128)(2,1)S(1)}, bf16[8,7168]{1,0:T(8,128)(2,1)S(1)}, u32[]{:S(2)}, u32[]{:S(2)}) collective-permute-start(bf16[8,7168]{1,0:T(8,128)(2,1)S(1)} %collective-permute-done.1.refs_1_), channel_id=1, source_target_pairs={{0,1},{1,0},{2,3},{3,2},{4,5},{5,4},{6,7},{7,6},{8,9},{9,8},{10,11... | collective-permute-start | bytes 344072 | tf_op jit(solution)/shard_map/ppermute | solution.py:333
  20.2 1.4 %collective-permute-start.6 = (bf16[8,7168]{1,0:T(8,128)(2,1)S(1)}, bf16[8,7168]{1,0:T(8,128)(2,1)S(1)}, u32[]{:S(2)}, u32[]{:S(2)}) collective-permute-start(bf16[8,7168]{1,0:T(8,128)(2,1)S(1)} %collective-permute-done.2.refs_2_), channel_id=1, source_target_pairs={{0,1},{1,0},{2,3},{3,2},{4,5},{5,4},{6,7},{7,6},{8,9},{9,8},{10,11... | collective-permute-start | bytes 344072 | tf_op jit(solution)/shard_map/ppermute | solution.py:333
  20.3 1.3 %collective-permute-start.7 = (bf16[8,3584]{1,0:T(8,128)(2,1)S(1)}, bf16[8,3584]{1,0:T(8,128)(2,1)S(1)}, u32[]{:S(2)}, u32[]{:S(2)}) collective-permute-start(bf16[8,3584]{1,0:T(8,128)(2,1)S(1)} %collective-permute-done.3.refs_6_), channel_id=1, source_target_pairs={{0,1},{1,0},{2,3},{3,2},{4,5},{5,4},{6,7},{7,6},{8,9},{9,8},{10,11... | collective-permute-start | bytes 172040 | tf_op jit(solution)/shard_map/ppermute | solution.py:334
  34.9 18.4 %copy-start = (s32[16,3]{0,1:T(4,128)S(1)}, s32[16,3]{0,1:T(4,128)}, u32[]{:S(2)}) copy-start(s32[16,3]{0,1:T(4,128)} %param.15) | copy-start | bytes 580
  34.9 18.4 %copy-start.1 = (s32[16,3]{0,1:T(4,128)S(1)}, s32[16,3]{0,1:T(4,128)}, u32[]{:S(2)}) copy-start(s32[16,3]{0,1:T(4,128)} %param.16) | copy-start | bytes 580
  34.9 1.9 %collective-permute-start.8 = (bf16[32,7168]{1,0:T(8,128)(2,1)S(1)}, bf16[32,7168]{1,0:T(8,128)(2,1)S(1)}, u32[]{:S(2)}, u32[]{:S(2)}) collective-permute-start(bf16[32,7168]{1,0:T(8,128)(2,1)S(1)} %get-tuple-element.68), channel_id=1, source_target_pairs={{0,1},{1,0},{2,3},{3,2},{4,5},{5,4},{6,7},{7,6},{8,9},{9,8},{10,11... | collective-permute-start | bytes 1376264 | tf_op jit(solution)/shard_map/ppermute | solution.py:366
  36.9 11.9 %collective-permute-start.9 = (bf16[8,7168]{1,0:T(8,128)(2,1)S(1)}, bf16[8,7168]{1,0:T(8,128)(2,1)S(1)}, u32[]{:S(2)}, u32[]{:S(2)}) collective-permute-start(bf16[8,7168]{1,0:T(8,128)(2,1)S(1)} %get-tuple-element.69), channel_id=1, source_target_pairs={{0,8},{1,13},{2,10},{3,15},{4,12},{5,9},{6,14},{7,11},{8,0},{9,5},... | collective-permute-start | bytes 344072 | tf_op jit(solution)/shard_map/ppermute | solution.py:376
  39.9 11.6 %collective-permute-start.10 = (bf16[8,7168]{1,0:T(8,128)(2,1)S(1)}, bf16[8,7168]{1,0:T(8,128)(2,1)S(1)}, u32[]{:S(2)}, u32[]{:S(2)}) collective-permute-start(bf16[8,7168]{1,0:T(8,128)(2,1)S(1)} %get-tuple-element.70), channel_id=1, source_target_pairs={{0,10},{1,15},{2,8},{3,13},{4,14},{5,11},{6,12},{7,9},{8,2},{9,7},... | collective-permute-start | bytes 344072 | tf_op jit(solution)/shard_map/ppermute | solution.py:376
  40.8 10.7 %collective-permute-start.11 = (bf16[8,7168]{1,0:T(8,128)(2,1)S(1)}, bf16[8,7168]{1,0:T(8,128)(2,1)S(1)}, u32[]{:S(2)}, u32[]{:S(2)}) collective-permute-start(bf16[8,7168]{1,0:T(8,128)(2,1)S(1)} %get-tuple-element.71), channel_id=1, source_target_pairs={{0,4},{1,7},{2,6},{3,5},{4,0},{5,3},{6,2},{7,1},{8,12},{9,15},{10,... | collective-permute-start | bytes 344072 | tf_op jit(solution)/shard_map/ppermute | solution.py:376
  41.3 5.9 %collective-permute-start.12 = (bf16[8,3584]{1,0:T(8,128)(2,1)S(1)}, bf16[8,3584]{1,0:T(8,128)(2,1)S(1)}, u32[]{:S(2)}, u32[]{:S(2)}) collective-permute-start(bf16[8,3584]{1,0:T(8,128)(2,1)S(1)} %get-tuple-element.72), channel_id=1, source_target_pairs={{0,2},{1,3},{2,0},{3,1},{4,6},{5,7},{6,4},{7,5},{8,10},{9,11},{10,... | collective-permute-start | bytes 172040 | tf_op jit(solution)/shard_map/ppermute | solution.py:377
  51.5 1.3 %collective-permute-start.13 = (bf16[8,7168]{1,0:T(8,128)(2,1)S(1)}, bf16[8,7168]{1,0:T(8,128)(2,1)S(1)}, u32[]{:S(2)}, u32[]{:S(2)}) collective-permute-start(bf16[8,7168]{1,0:T(8,128)(2,1)S(1)} %collective-permute-done.9.refs_0_), channel_id=1, source_target_pairs={{0,1},{1,0},{2,3},{3,2},{4,5},{5,4},{6,7},{7,6},{8,9},{9,8},{10,11... | collective-permute-start | bytes 344072 | tf_op jit(solution)/shard_map/ppermute | solution.py:379
  51.5 1.5 %collective-permute-start.14 = (bf16[8,7168]{1,0:T(8,128)(2,1)S(1)}, bf16[8,7168]{1,0:T(8,128)(2,1)S(1)}, u32[]{:S(2)}, u32[]{:S(2)}) collective-permute-start(bf16[8,7168]{1,0:T(8,128)(2,1)S(1)} %collective-permute-done.10.refs_1_), channel_id=1, source_target_pairs={{0,1},{1,0},{2,3},{3,2},{4,5},{5,4},{6,7},{7,6},{8,9},{9,8},{10,11... | collective-permute-start | bytes 344072 | tf_op jit(solution)/shard_map/ppermute | solution.py:379
  52.0 1.3 %collective-permute-start.15 = (bf16[8,7168]{1,0:T(8,128)(2,1)S(1)}, bf16[8,7168]{1,0:T(8,128)(2,1)S(1)}, u32[]{:S(2)}, u32[]{:S(2)}) collective-permute-start(bf16[8,7168]{1,0:T(8,128)(2,1)S(1)} %collective-permute-done.11.refs_2_), channel_id=1, source_target_pairs={{0,1},{1,0},{2,3},{3,2},{4,5},{5,4},{6,7},{7,6},{8,9},{9,8},{10,11... | collective-permute-start | bytes 344072 | tf_op jit(solution)/shard_map/ppermute | solution.py:379

commit v4 on v3

--- a/solution.py
+++ b/solution.py
@@ -11,7 +11,7 @@
 EXPERTS = 8
 TOP = 3
 MIB = 2**20
-HEAD = 1024
+FIRST = 18
 AHEAD = 4
 SWAP = [(0, 1), (1, 0)]
 VMEM = pltpu.VMEM
@@ -34,23 +34,28 @@
     ]
 
 
-def attention_kernel(loads, *refs):
+def hold_kernel(loads, *refs):
     n = len(loads)
-    sources, weights, out_ref, held = refs[:4], refs[4:6], refs[6], refs[7 : 7 + n]
-    lengths_ref, q_ref, k_ref, v_ref, packed, mixed, own_sems, sems = refs[7 + n :]
+    weights, held, mark, sems = refs[:2], refs[-n - 2 : -2], refs[-2], refs[-1]
+    copies = [
+        pltpu.make_async_copy(weights[j].at[pl.ds(start, rows)], held[i], sems.at[i])
+        for i, (j, start, rows) in enumerate(loads)
+    ]
+    for copy in copies:
+        copy.start()
+    mark[...] = jnp.zeros_like(mark)
+    for copy in copies:
+        copy.wait()
+
+
+def attention_kernel(*refs):
+    sources, out_ref = refs[:4], refs[4]
+    lengths_ref, q_ref, k_ref, v_ref, packed, mixed, own_sems = refs[5:]
     own = [
         pltpu.make_async_copy(source, ref, own_sems.at[i])
         for i, (source, ref) in enumerate(zip(sources, (lengths_ref, q_ref, k_ref, v_ref)))
     ]
     for copy in own:
-        copy.start()
-    copies = []
-    for i, (which, start, rows) in enumerate(loads):
-        copy = pltpu.make_async_copy(
-            weights[which].at[pl.ds(start, rows)], held[i], sems.at[i]
-        )
-        copies.append(copy)
-    for copy in copies[:AHEAD]:
         copy.start()
     requests, slots, size = k_ref.shape
     heads = q_ref.shape[1] // size
@@ -64,8 +69,6 @@
         )
     own[2].wait()
     own[3].wait()
-    for copy in copies[AHEAD:]:
-        copy.start()
     for r in range(requests):
         every = pl.ds(r, heads, stride=requests)
         query = jnp.concatenate([packed[j, every, :] for j in range(planes)], axis=1).astype(BF16)
@@ -84,8 +87,6 @@
         out_ref[:, i * 128 : (i + 1) * 128] = mixed[
             j, h * requests : (h + 1) * requests, :
         ].astype(BF16)
-    for copy in copies:
-        copy.wait()
 
 
 def places(routes, levels, ks, span, capacity):
@@ -149,28 +150,28 @@
     held = sum(i >= 0 for ranges in plan for _, _, i in ranges)
     at = 2 * m + 3
     parts_held, refs = refs[at : at + held], refs[at + held :]
-    gate_hbm, up_hbm, down_hbm, keep, give = refs[:5]
-    x, rest_w, down_w, total, result, hidden, rest_sem, down_sem = refs[5:]
+    gate_hbm, up_hbm, down_hbm = refs[:3]
+    keep, give, x, rest_w, down_w, total, result, hidden, rest_sem, down_sem = refs[-10:]
     core = lax.axis_index("tp")
     depth, width = x.shape[1], hidden.shape[1]
     half = depth // 2
     wide, ring = down_w.shape[1], down_w.shape[0]
     parts = width // wide
 
-    fetches, place = {}, 0
+    fetches, slots = {}, rest_w.shape[0]
     for ranges in zip(*plan):
         for j, (start, rows, i) in enumerate(ranges):
             source = (gate_hbm, up_hbm)[j]
             if i < 0:
+                place = len(fetches) % slots
                 fetches[j, start] = (
                     place,
                     pltpu.make_async_copy(
                         source.at[pl.ds(start, rows)],
-                        rest_w.at[pl.ds(place, rows)],
+                        rest_w.at[place],
                         rest_sem.at[len(fetches)],
                     ),
                 )
-                place += rows
 
     def fetch(i):
         return pltpu.make_async_copy(
@@ -199,7 +200,7 @@
                 place, copy = fetches[j, start]
                 copy.wait()
                 ask(1)
-                weight = rest_w[place : place + rows, :]
+                weight = rest_w[place]
             else:
                 weight = parts_held[i][...]
             term = jnp.dot(x[:, start : start + rows], weight, preferred_element_type=F32)
@@ -291,52 +292,44 @@
     total_rows = count * capacity
     step = width // 14
     roomy = total_rows <= 64
-    loads, plan = [], ([], [])
-    for j, early in enumerate((width, HEAD) if roomy else (0, 0)):
-        for start in range(0, width, step):
-            index = -1
-            if start < early:
-                index = len(loads)
-                loads.append((j, start, step))
-            plan[j].append((start, step, index))
+    order = [(j, start, step) for j in range(2) for start in range(0, width, step)]
+    first = loads = order[:FIRST] if roomy else []
+    plan = [
+        [(start, step, loads.index((j, start, step)) if (j, start, step) in loads else -1)
+         for start in range(0, width, step)]
+        for j in range(2)
+    ]
     gate_hbm, up_hbm, down_hbm = (far(w[0]) for w in (w_gate, w_up, w_down))
-    requests, slots, size = keys.shape
-    heads = queries.shape[1] // size
     in_hbm = pl.BlockSpec(memory_space=pltpu.HBM)
-    early_bytes = 4 * requests * slots * size + 2 * hid * step * len(loads)
-    context, *held = pl.pallas_call(
-        functools.partial(attention_kernel, loads),
-        out_shape=[jax.ShapeDtypeStruct(queries.shape, BF16)]
-        + [VMEM((rows, hid), BF16) for _, _, rows in loads],
-        in_specs=[in_hbm] * 6,
-        out_specs=[in_vmem] * (1 + len(loads)),
-        scratch_shapes=[
-            pltpu.SMEM(lengths.shape, jnp.int32),
-            VMEM(queries.shape, BF16),
-            VMEM(keys.shape, BF16),
-            VMEM(values.shape, BF16),
-            VMEM((size // 128, heads * requests, 128), F32),
-            VMEM((size // 128, heads * requests, 128), F32),
-            pltpu.SemaphoreType.DMA((4,)),
-            pltpu.SemaphoreType.DMA((max(1, len(loads)),)),
-        ],
-        compiler_params=pltpu.CompilerParams(vmem_limit_bytes=10 * MIB),
-        cost_estimate=pl.CostEstimate(
-            flops=4 * requests * heads * slots * size,
-            bytes_accessed=early_bytes,
-            transcendentals=requests * heads * slots,
-        ),
-        name="attention",
-    )(far(lengths), far(queries), far(keys), far(values), gate_hbm, up_hbm)
-
-    *mine, share_mine, context = lax.optimization_barrier((*mine, share_mine, context))
+
+    def hold(blocks):
+        *held, mark = pl.pallas_call(
+            functools.partial(hold_kernel, blocks),
+            out_shape=[VMEM((rows, hid), BF16) for _, _, rows in blocks]
+            + [jax.ShapeDtypeStruct((8, 128), F32)],
+            in_specs=[in_hbm] * 2,
+            out_specs=[in_vmem] * (len(blocks) + 1),
+            scratch_shapes=[pltpu.SemaphoreType.DMA((len(blocks),))],
+            compiler_params=pltpu.CompilerParams(vmem_limit_bytes=MIB),
+            cost_estimate=pl.CostEstimate(
+                flops=0, bytes_accessed=2 * hid * step * len(blocks), transcendentals=0
+            ),
+            name="hold",
+        )(gate_hbm, up_hbm)
+        return held, mark
+
+    held, marks = [], []
+    if first:
+        held, mark = hold(first)
+        *mine, share_mine, mark = lax.optimization_barrier((*mine, share_mine, mark))
+        marks = [mark]
     theirs = [lax.ppermute(b, "tp", SWAP) for b in mine]
     share_theirs = lax.ppermute(share_mine, "tp", SWAP)
 
     fetched = 2 * 14 - len(loads)
     wide = 256 if hid % 256 == 0 else hid
     parts = hid // wide
-    ring = min(parts, 3)
+    ring = min(parts, 5)
     weight_bytes = 2 * hid * (step * fetched + width)
     keep, give = pl.pallas_call(
         functools.partial(expert_kernel, m, capacity, plan),
@@ -344,11 +337,13 @@
             jax.ShapeDtypeStruct(((m + 1) * capacity, width), F32),
             jax.ShapeDtypeStruct(((m + 1) * capacity, width), BF16),
         ],
-        in_specs=[in_vmem] * (2 * m + 3 + len(held)) + [in_hbm] * 3,
+        in_specs=[in_vmem] * (2 * m + 3 + len(held))
+        + [in_hbm] * 3
+        + [pl.BlockSpec(memory_space=pl.ANY)] * len(marks),
         out_specs=[in_vmem] * 2,
         scratch_shapes=[
             VMEM((total_rows, width), BF16),
-            VMEM((step * fetched, hid), BF16),
+            VMEM((min(fetched, AHEAD + 1), step, hid), BF16),
             VMEM((ring, wide, width), BF16),
             VMEM((2, total_rows, hid), F32),
             VMEM((total_rows, width), F32),
@@ -356,12 +351,12 @@
             pltpu.SemaphoreType.DMA((fetched,)),
             pltpu.SemaphoreType.DMA((parts,)),
         ],
-        compiler_params=pltpu.CompilerParams(vmem_limit_bytes=(31 if roomy else 58) * MIB),
+        compiler_params=pltpu.CompilerParams(vmem_limit_bytes=(28 if roomy else 58) * MIB),
         cost_estimate=pl.CostEstimate(
             flops=2 * total_rows * 3 * width * hid, bytes_accessed=weight_bytes, transcendentals=0
         ),
         name="experts",
-    )(*mine, *theirs, share_mine, share_theirs, own, *held, gate_hbm, up_hbm, down_hbm)
+    )(*mine, *theirs, share_mine, share_theirs, own, *held, gate_hbm, up_hbm, down_hbm, *marks)
 
     got = lax.ppermute(give, "tp", SWAP)
     *back, share_back, own_back = pl.pallas_call(
@@ -375,7 +370,33 @@
 
     mine = [lax.ppermute(b, axes, route_of(count, pair)) for b, pair in zip(back, pairs)]
     share_back = lax.ppermute(share_back, axes, route_of(count, (1, 1)))
-    *mine, share_back = lax.optimization_barrier((*mine, share_back))
+
+    requests, slots, size = keys.shape
+    heads = queries.shape[1] // size
+    lengths, own_back = lax.optimization_barrier((lengths, own_back))
+    context = pl.pallas_call(
+        attention_kernel,
+        out_shape=jax.ShapeDtypeStruct(queries.shape, BF16),
+        in_specs=[in_hbm] * 4,
+        out_specs=in_vmem,
+        scratch_shapes=[
+            pltpu.SMEM(lengths.shape, jnp.int32),
+            VMEM(queries.shape, BF16),
+            VMEM(keys.shape, BF16),
+            VMEM(values.shape, BF16),
+            VMEM((size // 128, heads * requests, 128), F32),
+            VMEM((size // 128, heads * requests, 128), F32),
+            pltpu.SemaphoreType.DMA((4,)),
+        ],
+        compiler_params=pltpu.CompilerParams(vmem_limit_bytes=10 * MIB),
+        cost_estimate=pl.CostEstimate(
+            flops=4 * requests * heads * slots * size,
+            bytes_accessed=4 * requests * slots * size,
+            transcendentals=requests * heads * slots,
+        ),
+        name="attention",
+    )(far(lengths), far(queries), far(keys), far(values))
+    mine[0], share_back, context = lax.optimization_barrier((mine[0], share_back, context))
     theirs = [lax.ppermute(b, "tp", SWAP) for b in mine]
     moe_output = pl.pallas_call(
         functools.partial(combine_kernel, pairs, span, capacity),

time: 54.6 us -> 52 us (0.952)
  waiting for transfers between devices: 12.9 us -> 8.05 us
  Pallas kernels: 25.9 us -> 28.5 us
    ppermute x1, waiting for transfers between devices: 4.83 us -> 0.01 us  [body(): share_back = lax.ppermute(share_back, axes, route_of(count, (1, 1)))]
    pallas_call x1 -> x2, Pallas kernels: 10.1 us -> 12.7 us  [the longest x1 7.9 us: hold(): pl.pallas_call(functools.partial(hold_kernel, blocks), out_shape=[VMEM((r...]
  transfers between devices with their start and end apart: 16 -> 16, of which waited for: 8 -> 7; matrix products, arithmetic and copies ran while one was open for 0% -> 0% of each run, Pallas kernels for 19% -> 24%
where the time goes in v4:
time: 52 us; the launch traced here: 51.9 us
  Pallas kernels  28.5 us (55%)
  starting transfers between devices  14.6 us (28%)
  waiting for transfers between devices  8.05 us (15%)
  between operations  0.71 us (1%)
    pallas_call x1, Pallas kernels, body(): pl.pallas_call(functools.partial(expert_kernel, m, capacity, plan), out_s...  13.3 us
    ppermute x6, starting transfers between devices, body(): lax.ppermute(b, axes, route_of(count, pair))  11.1 us
    pallas_call x1, Pallas kernels, hold(): pl.pallas_call(functools.partial(hold_kernel, blocks), out_shape=[VMEM((r...  7.9 us
    pallas_call x1, Pallas kernels, body(): pl.pallas_call(attention_kernel, out_shape=jax.ShapeDtypeStruct(queries.s...  4.78 us
    ppermute x6, waiting for transfers between devices, body(): lax.ppermute(b, axes, route_of(count, pair))  4.7 us
    ppermute x1, waiting for transfers between devices, body(): got = lax.ppermute(give, 'tp', SWAP)  1.47 us
    pallas_call x1, Pallas kernels, body(): pl.pallas_call(functools.partial(dispatch_kernel, pairs, span, capacity),...  1.32 us
    pallas_call x1, Pallas kernels, body(): pl.pallas_call(functools.partial(combine_kernel, pairs, span, capacity),...  1.07 us
  transfers between devices with their start and end apart: 16, of which 7 were waited for; matrix products, arithmetic and copies ran while one was open for 0% of the time, Pallas kernels for 24%

profile of v4, /device:TPU:0, one launch (start us, length us, event | category | flops | bytes accessed | tf_op | source)
XLA Modules:
  0.0 51.9 jit_solution(10288443128958805605)
XLA Ops:
  0.6 1.3 %dispatch.1 = (bf16[8,7168]{1,0:T(8,128)(2,1)S(1)}, bf16[8,7168]{1,0:T(8,128)(2,1)S(1)}, bf16[8,7168]{1,0:T(8,128)(2,1)S(1)}, bf16[8,3584]{1,0:T(8,128)(2,1)S(1)}, bf16[8,7168]{1,0:T(8,128)(2,1)S(1)}) custom-call(s32[3,16]{1,0:T(4,128)} %bitcast.5, bf16[16,7168]{1,0:T(8,128)(2,1)} %x_hbm.1), custom_call_target="tpu_custom_call" | custom-call | tf_op jit(solution)/shard_map/dispatch/pallas_call | solution.py:276
  2.0 4.1 %collective-permute-start = (bf16[8,7168]{1,0:T(8,128)(2,1)S(1)}, bf16[8,7168]{1,0:T(8,128)(2,1)S(1)}, u32[]{:S(2)}, u32[]{:S(2)}) collective-permute-start(bf16[8,7168]{1,0:T(8,128)(2,1)S(1)} %get-tuple-element.43), channel_id=1, source_target_pairs={{0,8},{1,13},{2,10},{3,15},{4,12},{5,9},{6,14},{7,11},{8,0},{9,5},... | collective-permute-start | bytes 344072 | tf_op jit(solution)/shard_map/ppermute | solution.py:290
  6.1 1.3 %collective-permute-start.1 = (bf16[8,7168]{1,0:T(8,128)(2,1)S(1)}, bf16[8,7168]{1,0:T(8,128)(2,1)S(1)}, u32[]{:S(2)}, u32[]{:S(2)}) collective-permute-start(bf16[8,7168]{1,0:T(8,128)(2,1)S(1)} %get-tuple-element.44), channel_id=1, source_target_pairs={{0,10},{1,15},{2,8},{3,13},{4,14},{5,11},{6,12},{7,9},{8,2},{9,7},... | collective-permute-start | bytes 344072 | tf_op jit(solution)/shard_map/ppermute | solution.py:290
  7.3 1.6 %collective-permute-start.2 = (bf16[8,7168]{1,0:T(8,128)(2,1)S(1)}, bf16[8,7168]{1,0:T(8,128)(2,1)S(1)}, u32[]{:S(2)}, u32[]{:S(2)}) collective-permute-start(bf16[8,7168]{1,0:T(8,128)(2,1)S(1)} %get-tuple-element.45), channel_id=1, source_target_pairs={{0,4},{1,7},{2,6},{3,5},{4,0},{5,3},{6,2},{7,1},{8,12},{9,15},{10,... | collective-permute-start | bytes 344072 | tf_op jit(solution)/shard_map/ppermute | solution.py:290
  8.9 0.5 %collective-permute-start.3 = (bf16[8,3584]{1,0:T(8,128)(2,1)S(1)}, bf16[8,3584]{1,0:T(8,128)(2,1)S(1)}, u32[]{:S(2)}, u32[]{:S(2)}) collective-permute-start(bf16[8,3584]{1,0:T(8,128)(2,1)S(1)} %get-tuple-element.46), channel_id=1, source_target_pairs={{0,2},{1,3},{2,0},{3,1},{4,6},{5,7},{6,4},{7,5},{8,10},{9,11},{10,... | collective-permute-start | bytes 172040 | tf_op jit(solution)/shard_map/ppermute | solution.py:291
  9.4 7.9 %hold.1 = (bf16[512,1280]{1,0:T(8,128)(2,1)S(1)}, bf16[512,1280]{1,0:T(8,128)(2,1)S(1)}, bf16[512,1280]{1,0:T(8,128)(2,1)S(1)}, bf16[512,1280]{1,0:T(8,128)(2,1)...) custom-call(bf16[7168,1280]{1,0:T(8,128)(2,1)} %bitcast.8, ...), custom_call_target="tpu_custom_call" | custom-call | bytes 23592960 | tf_op jit(solution)/shard_map/hold/pallas_call | solution.py:306
  17.3 0.0 collective-permute-done.3.refs_6_
  17.4 0.3 collective-permute-done.1.refs_1_
  17.7 0.0 collective-permute-done.2.refs_2_
  17.7 0.0 collective-permute-start.4
  17.7 0.5 collective-permute-start.5
  18.2 0.0 collective-permute-start.6
  18.2 0.5 collective-permute-start.7
  18.7 0.9 %collective-permute-done.7.refs_7_ = bf16[8,3584]{1,0:T(8,128)(2,1)S(1)} collective-permute-done((bf16[8,3584]{1,0:T(8,128)(2,1)S(1)}, bf16[8,3584]{1,0:T(8,128)(2,1)S(1)}, u32[]{:S(2)}, u32[]{:S(2)}) %collective-permute-start.7) | collective-permute-done | bytes 57376 | tf_op jit(solution)/shard_map/ppermute | solution.py:327
  19.6 0.0 collective-permute-done.4.refs_3_
  19.6 13.3 %experts.1 = (f32[32,7168]{1,0:T(8,128)S(1)}, bf16[32,7168]{1,0:T(8,128)(2,1)S(1)}) custom-call(bf16[8,7168]{1,0:T(8,128)(2,1)S(1)} %collective-permute-done.refs_0_, bf16[8,7168]{1,0:T(8,128)(2,1)S(1)} %collective-permute-done.1.refs_1_, bf16[8,7168]{1,0:T(8,128)(2,1)S(1)} %collective-permute-done.2.refs_2_, ...), custom_call_target="tpu_custom_call" | custom-call | flops 3523215360 | bytes 31457280 | tf_op jit(solution)/shard_map/experts/pallas_call | solution.py:334
  32.9 0.4 collective-permute-start.8
  33.4 1.5 %collective-permute-done.8.got = bf16[32,7168]{1,0:T(8,128)(2,1)S(1)} collective-permute-done((bf16[32,7168]{1,0:T(8,128)(2,1)S(1)}, bf16[32,7168]{1,0:T(8,128)(2,1)S(1)}, u32[]{:S(2)}, u32[]{:S(2)}) %collective-permute-start.8) | collective-permute-done | bytes 458784 | tf_op jit(solution)/shard_map/ppermute | solution.py:361
  34.8 0.1 sum.1
  34.9 2.8 %collective-permute-start.9 = (bf16[8,7168]{1,0:T(8,128)(2,1)S(1)}, bf16[8,7168]{1,0:T(8,128)(2,1)S(1)}, u32[]{:S(2)}, u32[]{:S(2)}) collective-permute-start(bf16[8,7168]{1,0:T(8,128)(2,1)S(1)} %get-tuple-element.74), channel_id=1, source_target_pairs={{0,8},{1,13},{2,10},{3,15},{4,12},{5,9},{6,14},{7,11},{8,0},{9,5},... | collective-permute-start | bytes 344072 | tf_op jit(solution)/shard_map/ppermute | solution.py:371
  37.7 0.9 %collective-permute-start.11 = (bf16[8,7168]{1,0:T(8,128)(2,1)S(1)}, bf16[8,7168]{1,0:T(8,128)(2,1)S(1)}, u32[]{:S(2)}, u32[]{:S(2)}) collective-permute-start(bf16[8,7168]{1,0:T(8,128)(2,1)S(1)} %get-tuple-element.80), channel_id=1, source_target_pairs={{0,10},{1,15},{2,8},{3,13},{4,14},{5,11},{6,12},{7,9},{8,2},{9,7},... | collective-permute-start | bytes 344072 | tf_op jit(solution)/shard_map/ppermute | solution.py:371
  38.6 0.4 collective-permute-start.12
  39.1 1.0 %collective-permute-start.10 = (bf16[8,3584]{1,0:T(8,128)(2,1)S(1)}, bf16[8,3584]{1,0:T(8,128)(2,1)S(1)}, u32[]{:S(2)}, u32[]{:S(2)}) collective-permute-start(bf16[8,3584]{1,0:T(8,128)(2,1)S(1)} %get-tuple-element.75), channel_id=1, source_target_pairs={{0,2},{1,3},{2,0},{3,1},{4,6},{5,7},{6,4},{7,5},{8,10},{9,11},{10,... | collective-permute-start | bytes 172040 | tf_op jit(solution)/shard_map/ppermute | solution.py:372
  40.1 4.8 %attention.1 = bf16[4,8192]{1,0:T(4,128)(2,1)} custom-call(s32[4]{0:T(128)} %refs_0_, bf16[4,8192]{1,0:T(4,128)(2,1)} %refs_1_.1, bf16[4,1024,256]{2,1,0:T(8,128)(2,1)} %refs_2_.1, bf16[4,1024,256]{2,1,0:T(8,128)(2,1)} %refs_3_.1), custom_call_target="tpu_custom_call" | custom-call | flops 134217728 | bytes 4194304 | tf_op jit(solution)/shard_map/attention/pallas_call | solution.py:377
  44.9 1.9 %collective-permute-done.9.refs_0_ = bf16[8,7168]{1,0:T(8,128)(2,1)S(1)} collective-permute-done((bf16[8,7168]{1,0:T(8,128)(2,1)S(1)}, bf16[8,7168]{1,0:T(8,128)(2,1)S(1)}, u32[]{:S(2)}, u32[]{:S(2)}) %collective-permute-start.9) | collective-permute-done | bytes 114720 | tf_op jit(solution)/shard_map/ppermute | solution.py:371
  46.8 2.5 %collective-permute-done.11.refs_1_ = bf16[8,7168]{1,0:T(8,128)(2,1)S(1)} collective-permute-done((bf16[8,7168]{1,0:T(8,128)(2,1)S(1)}, bf16[8,7168]{1,0:T(8,128)(2,1)S(1)}, u32[]{:S(2)}, u32[]{:S(2)}) %collective-permute-start.11) | collective-permute-done | bytes 114720 | tf_op jit(solution)/shard_map/ppermute | solution.py:371
  49.3 0.0 collective-permute-start.14
  49.3 0.0 collective-permute-done.12.refs_2_
  49.3 0.5 collective-permute-start.15
  49.8 0.8 %collective-permute-done.14.refs_4_ = bf16[8,7168]{1,0:T(8,128)(2,1)S(1)} collective-permute-done((bf16[8,7168]{1,0:T(8,128)(2,1)S(1)}, bf16[8,7168]{1,0:T(8,128)(2,1)S(1)}, u32[]{:S(2)}, u32[]{:S(2)}) %collective-permute-start.14) | collective-permute-done | bytes 114720 | tf_op jit(solution)/shard_map/ppermute | solution.py:400
  50.6 0.2 collective-permute-done.15.refs_5_
  50.8 1.1 %combine.1 = bf16[16,3584]{1,0:T(8,128)(2,1)} custom-call(s32[3,16]{1,0:T(4,128)S(1)} %bitcast.6, s32[3,16]{1,0:T(4,128)S(1)} %bitcast.7, bf16[8,7168]{1,0:T(8,128)(2,1)S(1)} %collective-permute-done.9.refs_0_, bf16[8,7168]{1,0:T(8,128)(2,1)S(1)} %collective-permute-done.11.refs_1_, bf16[8,7168]{1,0:T(8,128)(2,1)S(1)} %collective-permute-done.12.refs_2_, ...), custom_call_target="tpu_custom_call" | custom-call | tf_op jit(solution)/shard_map/combine/pallas_call | solution.py:401
  (10 shorter events, 0.0 us)
Async XLA Ops:
  2.0 15.4 %collective-permute-start = (bf16[8,7168]{1,0:T(8,128)(2,1)S(1)}, bf16[8,7168]{1,0:T(8,128)(2,1)S(1)}, u32[]{:S(2)}, u32[]{:S(2)}) collective-permute-start(bf16[8,7168]{1,0:T(8,128)(2,1)S(1)} %get-tuple-element.43), channel_id=1, source_target_pairs={{0,8},{1,13},{2,10},{3,15},{4,12},{5,9},{6,14},{7,11},{8,0},{9,5},... | collective-permute-start | bytes 344072 | tf_op jit(solution)/shard_map/ppermute | solution.py:290
  6.1 11.6 %collective-permute-start.1 = (bf16[8,7168]{1,0:T(8,128)(2,1)S(1)}, bf16[8,7168]{1,0:T(8,128)(2,1)S(1)}, u32[]{:S(2)}, u32[]{:S(2)}) collective-permute-start(bf16[8,7168]{1,0:T(8,128)(2,1)S(1)} %get-tuple-element.44), channel_id=1, source_target_pairs={{0,10},{1,15},{2,8},{3,13},{4,14},{5,11},{6,12},{7,9},{8,2},{9,7},... | collective-permute-start | bytes 344072 | tf_op jit(solution)/shard_map/ppermute | solution.py:290
  7.3 10.3 %collective-permute-start.2 = (bf16[8,7168]{1,0:T(8,128)(2,1)S(1)}, bf16[8,7168]{1,0:T(8,128)(2,1)S(1)}, u32[]{:S(2)}, u32[]{:S(2)}) collective-permute-start(bf16[8,7168]{1,0:T(8,128)(2,1)S(1)} %get-tuple-element.45), channel_id=1, source_target_pairs={{0,4},{1,7},{2,6},{3,5},{4,0},{5,3},{6,2},{7,1},{8,12},{9,15},{10,... | collective-permute-start | bytes 344072 | tf_op jit(solution)/shard_map/ppermute | solution.py:290
  8.9 8.4 %collective-permute-start.3 = (bf16[8,3584]{1,0:T(8,128)(2,1)S(1)}, bf16[8,3584]{1,0:T(8,128)(2,1)S(1)}, u32[]{:S(2)}, u32[]{:S(2)}) collective-permute-start(bf16[8,3584]{1,0:T(8,128)(2,1)S(1)} %get-tuple-element.46), channel_id=1, source_target_pairs={{0,2},{1,3},{2,0},{3,1},{4,6},{5,7},{6,4},{7,5},{8,10},{9,11},{10,... | collective-permute-start | bytes 172040 | tf_op jit(solution)/shard_map/ppermute | solution.py:291
  17.7 1.9 %collective-permute-start.4 = (bf16[8,7168]{1,0:T(8,128)(2,1)S(1)}, bf16[8,7168]{1,0:T(8,128)(2,1)S(1)}, u32[]{:S(2)}, u32[]{:S(2)}) collective-permute-start(bf16[8,7168]{1,0:T(8,128)(2,1)S(1)} %collective-permute-done.refs_0_), channel_id=1, source_target_pairs={{0,1},{1,0},{2,3},{3,2},{4,5},{5,4},{6,7},{7,6},{8,9},{9,8},{10,11... | collective-permute-start | bytes 344072 | tf_op jit(solution)/shard_map/ppermute | solution.py:326
  17.7 1.9 %collective-permute-start.5 = (bf16[8,7168]{1,0:T(8,128)(2,1)S(1)}, bf16[8,7168]{1,0:T(8,128)(2,1)S(1)}, u32[]{:S(2)}, u32[]{:S(2)}) collective-permute-start(bf16[8,7168]{1,0:T(8,128)(2,1)S(1)} %collective-permute-done.1.refs_1_), channel_id=1, source_target_pairs={{0,1},{1,0},{2,3},{3,2},{4,5},{5,4},{6,7},{7,6},{8,9},{9,8},{10,11... | collective-permute-start | bytes 344072 | tf_op jit(solution)/shard_map/ppermute | solution.py:326
  18.2 1.4 %collective-permute-start.6 = (bf16[8,7168]{1,0:T(8,128)(2,1)S(1)}, bf16[8,7168]{1,0:T(8,128)(2,1)S(1)}, u32[]{:S(2)}, u32[]{:S(2)}) collective-permute-start(bf16[8,7168]{1,0:T(8,128)(2,1)S(1)} %collective-permute-done.2.refs_2_), channel_id=1, source_target_pairs={{0,1},{1,0},{2,3},{3,2},{4,5},{5,4},{6,7},{7,6},{8,9},{9,8},{10,11... | collective-permute-start | bytes 344072 | tf_op jit(solution)/shard_map/ppermute | solution.py:326
  18.2 1.4 %collective-permute-start.7 = (bf16[8,3584]{1,0:T(8,128)(2,1)S(1)}, bf16[8,3584]{1,0:T(8,128)(2,1)S(1)}, u32[]{:S(2)}, u32[]{:S(2)}) collective-permute-start(bf16[8,3584]{1,0:T(8,128)(2,1)S(1)} %collective-permute-done.3.refs_6_), channel_id=1, source_target_pairs={{0,1},{1,0},{2,3},{3,2},{4,5},{5,4},{6,7},{7,6},{8,9},{9,8},{10,11... | collective-permute-start | bytes 172040 | tf_op jit(solution)/shard_map/ppermute | solution.py:327
  32.9 1.9 %collective-permute-start.8 = (bf16[32,7168]{1,0:T(8,128)(2,1)S(1)}, bf16[32,7168]{1,0:T(8,128)(2,1)S(1)}, u32[]{:S(2)}, u32[]{:S(2)}) collective-permute-start(bf16[32,7168]{1,0:T(8,128)(2,1)S(1)} %get-tuple-element.73), channel_id=1, source_target_pairs={{0,1},{1,0},{2,3},{3,2},{4,5},{5,4},{6,7},{7,6},{8,9},{9,8},{10,11... | collective-permute-start | bytes 1376264 | tf_op jit(solution)/shard_map/ppermute | solution.py:361
  34.9 11.9 %collective-permute-start.9 = (bf16[8,7168]{1,0:T(8,128)(2,1)S(1)}, bf16[8,7168]{1,0:T(8,128)(2,1)S(1)}, u32[]{:S(2)}, u32[]{:S(2)}) collective-permute-start(bf16[8,7168]{1,0:T(8,128)(2,1)S(1)} %get-tuple-element.74), channel_id=1, source_target_pairs={{0,8},{1,13},{2,10},{3,15},{4,12},{5,9},{6,14},{7,11},{8,0},{9,5},... | collective-permute-start | bytes 344072 | tf_op jit(solution)/shard_map/ppermute | solution.py:371
  37.7 11.6 %collective-permute-start.11 = (bf16[8,7168]{1,0:T(8,128)(2,1)S(1)}, bf16[8,7168]{1,0:T(8,128)(2,1)S(1)}, u32[]{:S(2)}, u32[]{:S(2)}) collective-permute-start(bf16[8,7168]{1,0:T(8,128)(2,1)S(1)} %get-tuple-element.80), channel_id=1, source_target_pairs={{0,10},{1,15},{2,8},{3,13},{4,14},{5,11},{6,12},{7,9},{8,2},{9,7},... | collective-permute-start | bytes 344072 | tf_op jit(solution)/shard_map/ppermute | solution.py:371
  38.6 10.7 %collective-permute-start.12 = (bf16[8,7168]{1,0:T(8,128)(2,1)S(1)}, bf16[8,7168]{1,0:T(8,128)(2,1)S(1)}, u32[]{:S(2)}, u32[]{:S(2)}) collective-permute-start(bf16[8,7168]{1,0:T(8,128)(2,1)S(1)} %get-tuple-element.81), channel_id=1, source_target_pairs={{0,4},{1,7},{2,6},{3,5},{4,0},{5,3},{6,2},{7,1},{8,12},{9,15},{10,... | collective-permute-start | bytes 344072 | tf_op jit(solution)/shard_map/ppermute | solution.py:371
  39.1 5.8 %collective-permute-start.10 = (bf16[8,3584]{1,0:T(8,128)(2,1)S(1)}, bf16[8,3584]{1,0:T(8,128)(2,1)S(1)}, u32[]{:S(2)}, u32[]{:S(2)}) collective-permute-start(bf16[8,3584]{1,0:T(8,128)(2,1)S(1)} %get-tuple-element.75), channel_id=1, source_target_pairs={{0,2},{1,3},{2,0},{3,1},{4,6},{5,7},{6,4},{7,5},{8,10},{9,11},{10,... | collective-permute-start | bytes 172040 | tf_op jit(solution)/shard_map/ppermute | solution.py:372
  40.1 10.7 %copy-start = (s32[16,3]{0,1:T(4,128)S(1)}, s32[16,3]{0,1:T(4,128)}, u32[]{:S(2)}) copy-start(s32[16,3]{0,1:T(4,128)} %param.15) | copy-start | bytes 580
  40.1 10.7 %copy-start.1 = (s32[16,3]{0,1:T(4,128)S(1)}, s32[16,3]{0,1:T(4,128)}, u32[]{:S(2)}) copy-start(s32[16,3]{0,1:T(4,128)} %param.16) | copy-start | bytes 580
  46.8 3.1 %collective-permute-start.13 = (bf16[8,7168]{1,0:T(8,128)(2,1)S(1)}, bf16[8,7168]{1,0:T(8,128)(2,1)S(1)}, u32[]{:S(2)}, u32[]{:S(2)}) collective-permute-start(bf16[8,7168]{1,0:T(8,128)(2,1)S(1)} %collective-permute-done.9.refs_0_), channel_id=1, source_target_pairs={{0,1},{1,0},{2,3},{3,2},{4,5},{5,4},{6,7},{7,6},{8,9},{9,8},{10,11... | collective-permute-start | bytes 344072 | tf_op jit(solution)/shard_map/ppermute | solution.py:400
  49.3 1.3 %collective-permute-start.14 = (bf16[8,7168]{1,0:T(8,128)(2,1)S(1)}, bf16[8,7168]{1,0:T(8,128)(2,1)S(1)}, u32[]{:S(2)}, u32[]{:S(2)}) collective-permute-start(bf16[8,7168]{1,0:T(8,128)(2,1)S(1)} %collective-permute-done.11.refs_1_), channel_id=1, source_target_pairs={{0,1},{1,0},{2,3},{3,2},{4,5},{5,4},{6,7},{7,6},{8,9},{9,8},{10,11... | collective-permute-start | bytes 344072 | tf_op jit(solution)/shard_map/ppermute | solution.py:400
  49.3 1.5 %collective-permute-start.15 = (bf16[8,7168]{1,0:T(8,128)(2,1)S(1)}, bf16[8,7168]{1,0:T(8,128)(2,1)S(1)}, u32[]{:S(2)}, u32[]{:S(2)}) collective-permute-start(bf16[8,7168]{1,0:T(8,128)(2,1)S(1)} %collective-permute-done.12.refs_2_), channel_id=1, source_target_pairs={{0,1},{1,0},{2,3},{3,2},{4,5},{5,4},{6,7},{7,6},{8,9},{9,8},{10,11... | collective-permute-start | bytes 344072 | tf_op jit(solution)/shard_map/ppermute | solution.py:400

commit v5 on v4

--- a/solution.py
+++ b/solution.py
@@ -48,9 +48,9 @@
         copy.wait()
 
 
-def attention_kernel(*refs):
-    sources, out_ref = refs[:4], refs[4]
-    lengths_ref, q_ref, k_ref, v_ref, packed, mixed, own_sems = refs[5:]
+def attention_kernel(pairs, span, capacity, routes_ref, level_ref, *refs):
+    sources, out_ref, gates_ref = refs[:4], refs[4], refs[5]
+    lengths_ref, q_ref, k_ref, v_ref, packed, mixed, own_sems = refs[6:]
     own = [
         pltpu.make_async_copy(source, ref, own_sems.at[i])
         for i, (source, ref) in enumerate(zip(sources, (lengths_ref, q_ref, k_ref, v_ref)))
@@ -87,6 +87,13 @@
         out_ref[:, i * 128 : (i + 1) * 128] = mixed[
             j, h * requests : (h + 1) * requests, :
         ].astype(BF16)
+    core = lax.axis_index("tp")
+    ks = [jnp.where(core == 0, a, b) for a, b in pairs]
+    ks += [jnp.where(core == 0, b, a) for a, b in pairs] + [1, 0]
+    here, level = places(routes_ref[...], level_ref[...], ks, span, capacity)
+    weight = jnp.where(here, level, 0).astype(F32) / 1024.0
+    high = weight.astype(BF16).astype(F32)
+    gates_ref[...] = jnp.concatenate([high, weight - high], axis=1).T.astype(BF16)
 
 
 def places(routes, levels, ks, span, capacity):
@@ -178,7 +185,18 @@
             down_hbm.at[pl.ds(i * wide, wide)], down_w.at[i % ring], down_sem.at[i]
         )
 
-    queue = [copy for _, copy in fetches.values()] + [fetch(i) for i in range(min(ring, parts))]
+    def fetch_last(c):
+        at, rows = pl.ds(c * half, half), pl.ds((parts - 1) * wide, wide)
+        return pltpu.make_async_copy(
+            down_hbm.at[rows, at], down_w.at[(parts - 1) % ring, :, at], down_sem.at[parts - 1 + c]
+        )
+
+    def fetches_of(i):
+        return [fetch(i)] if i < parts - 1 else [fetch_last(0), fetch_last(1)]
+
+    queue = [copy for _, copy in fetches.values()]
+    for i in range(min(ring, parts)):
+        queue += fetches_of(i)
 
     def ask(number):
         for copy in queue[:number]:
@@ -208,14 +226,24 @@
     ask(len(queue))
     gate = total[0]
     hidden[...] = (gate / (1.0 + jnp.exp(-gate)) * total[1]).astype(BF16)
-    for i in range(parts):
+    for i in range(parts - 1):
         fetch(i).wait()
         term = jnp.dot(
             hidden[:, i * wide : (i + 1) * wide], down_w[i % ring], preferred_element_type=F32
         )
         result[...] = term if i == 0 else result[...] + term
         if i + ring < parts:
-            fetch(i + ring).start()
+            for copy in fetches_of(i + ring):
+                copy.start()
+    for c in range(2):
+        fetch_last(c).wait()
+        at = slice(c * half, (c + 1) * half)
+        term = jnp.dot(
+            hidden[:, (parts - 1) * wide :],
+            down_w[(parts - 1) % ring, :, at],
+            preferred_element_type=F32,
+        )
+        result[:, at] = term if parts == 1 else result[:, at] + term
     n = m * capacity
     keep[:n, :] = result[:n, :]
     mine = pl.ds(pl.multiple_of(core * half, 128), half)
@@ -237,24 +265,14 @@
     outs[m + 1][...] = both[m * capacity :, half:].astype(BF16)
 
 
-def combine_kernel(pairs, span, capacity, routes_ref, level_ref, *refs):
-    m = len(pairs)
-    blocks, shared, own, out = refs[: 2 * m], refs[2 * m], refs[2 * m + 1], refs[2 * m + 2]
+def combine_kernel(gates_ref, *refs):
+    *blocks, shared, own, out = refs
     core = lax.axis_index("tp")
-    half = out.shape[1]
-    ks = [jnp.where(core == 0, a, b) for a, b in pairs]
-    ks += [jnp.where(core == 0, b, a) for a, b in pairs] + [1, 0]
-    here, level = places(routes_ref[...], level_ref[...], ks, span, capacity)
-    weight = jnp.where(here, level, 0).astype(F32) / 1024.0
-    high = weight.astype(BF16)
-    low = (weight - high.astype(F32)).astype(BF16)
+    rows, half = out.shape
     at = pl.ds(pl.multiple_of(core * half, 128), half)
     held = jnp.concatenate([b[:, at] for b in blocks] + [shared[...], own[...]], axis=0)
-    dims = (((0,), (0,)), ((), ()))
-    out[...] = (
-        lax.dot_general(high, held, dims, preferred_element_type=F32)
-        + lax.dot_general(low, held, dims, preferred_element_type=F32)
-    ).astype(BF16)
+    both = jnp.dot(gates_ref[...], held, preferred_element_type=F32)
+    out[...] = (both[:rows] + both[rows:]).astype(BF16)
 
 
 def body(queries, keys, values, lengths, moe_input, routes, gate_level, w_gate, w_up, w_down):
@@ -349,7 +367,7 @@
             VMEM((total_rows, width), F32),
             VMEM((total_rows, hid), BF16),
             pltpu.SemaphoreType.DMA((fetched,)),
-            pltpu.SemaphoreType.DMA((parts,)),
+            pltpu.SemaphoreType.DMA((parts + 1,)),
         ],
         compiler_params=pltpu.CompilerParams(vmem_limit_bytes=(28 if roomy else 58) * MIB),
         cost_estimate=pl.CostEstimate(
@@ -374,11 +392,14 @@
     requests, slots, size = keys.shape
     heads = queries.shape[1] // size
     lengths, own_back = lax.optimization_barrier((lengths, own_back))
-    context = pl.pallas_call(
-        attention_kernel,
-        out_shape=jax.ShapeDtypeStruct(queries.shape, BF16),
-        in_specs=[in_hbm] * 4,
-        out_specs=in_vmem,
+    context, gates = pl.pallas_call(
+        functools.partial(attention_kernel, pairs, span, capacity),
+        out_shape=[
+            jax.ShapeDtypeStruct(queries.shape, BF16),
+            jax.ShapeDtypeStruct((2 * rows_here, total_rows), BF16),
+        ],
+        in_specs=[in_vmem] * 2 + [in_hbm] * 4,
+        out_specs=[in_vmem] * 2,
         scratch_shapes=[
             pltpu.SMEM(lengths.shape, jnp.int32),
             VMEM(queries.shape, BF16),
@@ -395,17 +416,17 @@
             transcendentals=requests * heads * slots,
         ),
         name="attention",
-    )(far(lengths), far(queries), far(keys), far(values))
+    )(routes_t, level_t, far(lengths), far(queries), far(keys), far(values))
     mine[0], share_back, context = lax.optimization_barrier((mine[0], share_back, context))
     theirs = [lax.ppermute(b, "tp", SWAP) for b in mine]
     moe_output = pl.pallas_call(
-        functools.partial(combine_kernel, pairs, span, capacity),
+        combine_kernel,
         out_shape=jax.ShapeDtypeStruct((rows_here, half), BF16),
-        in_specs=[in_vmem] * (2 * m + 4),
+        in_specs=[in_vmem] * (2 * m + 3),
         out_specs=in_vmem,
         compiler_params=pltpu.CompilerParams(vmem_limit_bytes=(8 if m < 8 else 40) * MIB),
         name="combine",
-    )(routes_t, level_t, *mine, *theirs, share_back, own_back)
+    )(gates, *mine, *theirs, share_back, own_back)
     return (context, moe_output)
 
 

time: 52 us -> 51.7 us (level)
  transfers between devices with their start and end apart: 16 -> 16, of which waited for: 7 -> 7; matrix products, arithmetic and copies ran while one was open for 0% -> 0% of each run, Pallas kernels for 24% -> 25%
where the time goes in v5:
time: 51.7 us; the launch traced here: 51.5 us
  Pallas kernels  28.2 us (55%)
  starting transfers between devices  14.6 us (28%)
  waiting for transfers between devices  7.97 us (15%)
  between operations  0.72 us (1%)
    pallas_call x1, Pallas kernels, body(): pl.pallas_call(functools.partial(expert_kernel, m, capacity, plan), out_s...  13.1 us
    ppermute x6, starting transfers between devices, body(): lax.ppermute(b, axes, route_of(count, pair))  11.1 us
    pallas_call x1, Pallas kernels, hold(): pl.pallas_call(functools.partial(hold_kernel, blocks), out_shape=[VMEM((r...  7.9 us
    pallas_call x1, Pallas kernels, body(): pl.pallas_call(functools.partial(attention_kernel, pairs, span, capacity)...  4.86 us
    ppermute x6, waiting for transfers between devices, body(): lax.ppermute(b, axes, route_of(count, pair))  4.62 us
    ppermute x1, waiting for transfers between devices, body(): got = lax.ppermute(give, 'tp', SWAP)  1.47 us
    pallas_call x1, Pallas kernels, body(): pl.pallas_call(functools.partial(dispatch_kernel, pairs, span, capacity),...  1.32 us
    ppermute x1, starting transfers between devices, body(): share_back = lax.ppermute(share_back, axes, route_of(count, (1, 1)))  1.05 us
  transfers between devices with their start and end apart: 16, of which 7 were waited for; matrix products, arithmetic and copies ran while one was open for 0% of the time, Pallas kernels for 25%

profile of v5, /device:TPU:0, one launch (start us, length us, event | category | flops | bytes accessed | tf_op | source)
XLA Modules:
  0.0 51.5 jit_solution(17447668338546169584)
XLA Ops:
  0.6 1.3 %dispatch.1 = (bf16[8,7168]{1,0:T(8,128)(2,1)S(1)}, bf16[8,7168]{1,0:T(8,128)(2,1)S(1)}, bf16[8,7168]{1,0:T(8,128)(2,1)S(1)}, bf16[8,3584]{1,0:T(8,128)(2,1)S(1)}, bf16[8,7168]{1,0:T(8,128)(2,1)S(1)}) custom-call(s32[3,16]{1,0:T(4,128)} %bitcast.5, bf16[16,7168]{1,0:T(8,128)(2,1)} %x_hbm.1), custom_call_target="tpu_custom_call" | custom-call | tf_op jit(solution)/shard_map/dispatch/pallas_call | solution.py:294
  2.0 4.1 %collective-permute-start = (bf16[8,7168]{1,0:T(8,128)(2,1)S(1)}, bf16[8,7168]{1,0:T(8,128)(2,1)S(1)}, u32[]{:S(2)}, u32[]{:S(2)}) collective-permute-start(bf16[8,7168]{1,0:T(8,128)(2,1)S(1)} %get-tuple-element.45), channel_id=1, source_target_pairs={{0,8},{1,13},{2,10},{3,15},{4,12},{5,9},{6,14},{7,11},{8,0},{9,5},... | collective-permute-start | bytes 344072 | tf_op jit(solution)/shard_map/ppermute | solution.py:308
  6.1 1.3 %collective-permute-start.1 = (bf16[8,7168]{1,0:T(8,128)(2,1)S(1)}, bf16[8,7168]{1,0:T(8,128)(2,1)S(1)}, u32[]{:S(2)}, u32[]{:S(2)}) collective-permute-start(bf16[8,7168]{1,0:T(8,128)(2,1)S(1)} %get-tuple-element.46), channel_id=1, source_target_pairs={{0,10},{1,15},{2,8},{3,13},{4,14},{5,11},{6,12},{7,9},{8,2},{9,7},... | collective-permute-start | bytes 344072 | tf_op jit(solution)/shard_map/ppermute | solution.py:308
  7.3 1.6 %collective-permute-start.2 = (bf16[8,7168]{1,0:T(8,128)(2,1)S(1)}, bf16[8,7168]{1,0:T(8,128)(2,1)S(1)}, u32[]{:S(2)}, u32[]{:S(2)}) collective-permute-start(bf16[8,7168]{1,0:T(8,128)(2,1)S(1)} %get-tuple-element.47), channel_id=1, source_target_pairs={{0,4},{1,7},{2,6},{3,5},{4,0},{5,3},{6,2},{7,1},{8,12},{9,15},{10,... | collective-permute-start | bytes 344072 | tf_op jit(solution)/shard_map/ppermute | solution.py:308
  8.9 0.5 %collective-permute-start.3 = (bf16[8,3584]{1,0:T(8,128)(2,1)S(1)}, bf16[8,3584]{1,0:T(8,128)(2,1)S(1)}, u32[]{:S(2)}, u32[]{:S(2)}) collective-permute-start(bf16[8,3584]{1,0:T(8,128)(2,1)S(1)} %get-tuple-element.48), channel_id=1, source_target_pairs={{0,2},{1,3},{2,0},{3,1},{4,6},{5,7},{6,4},{7,5},{8,10},{9,11},{10,... | collective-permute-start | bytes 172040 | tf_op jit(solution)/shard_map/ppermute | solution.py:309
  9.4 7.9 %hold.1 = (bf16[512,1280]{1,0:T(8,128)(2,1)S(1)}, bf16[512,1280]{1,0:T(8,128)(2,1)S(1)}, bf16[512,1280]{1,0:T(8,128)(2,1)S(1)}, bf16[512,1280]{1,0:T(8,128)(2,1)...) custom-call(bf16[7168,1280]{1,0:T(8,128)(2,1)} %bitcast.8, ...), custom_call_target="tpu_custom_call" | custom-call | bytes 23592960 | tf_op jit(solution)/shard_map/hold/pallas_call | solution.py:324
  17.4 0.3 collective-permute-done.1.refs_1_
  17.7 0.5 collective-permute-start.5
  18.2 0.0 collective-permute-start.6
  18.2 0.5 collective-permute-start.7
  18.7 0.9 %collective-permute-done.7.refs_7_ = bf16[8,3584]{1,0:T(8,128)(2,1)S(1)} collective-permute-done((bf16[8,3584]{1,0:T(8,128)(2,1)S(1)}, bf16[8,3584]{1,0:T(8,128)(2,1)S(1)}, u32[]{:S(2)}, u32[]{:S(2)}) %collective-permute-start.7) | collective-permute-done | bytes 57376 | tf_op jit(solution)/shard_map/ppermute | solution.py:345
  19.6 0.0 collective-permute-done.4.refs_3_
  19.6 0.0 collective-permute-done.5.refs_4_
  19.6 0.0 collective-permute-done.6.refs_5_
  19.6 13.1 %experts.1 = (f32[32,7168]{1,0:T(8,128)S(1)}, bf16[32,7168]{1,0:T(8,128)(2,1)S(1)}) custom-call(bf16[8,7168]{1,0:T(8,128)(2,1)S(1)} %collective-permute-done.refs_0_, bf16[8,7168]{1,0:T(8,128)(2,1)S(1)} %collective-permute-done.1.refs_1_, bf16[8,7168]{1,0:T(8,128)(2,1)S(1)} %collective-permute-done.2.refs_2_, ...), custom_call_target="tpu_custom_call" | custom-call | flops 3523215360 | bytes 31457280 | tf_op jit(solution)/shard_map/experts/pallas_call | solution.py:352
  32.7 0.0 copy-start
  32.8 0.0 copy-start.1
  32.8 0.4 collective-permute-start.8
  33.2 1.5 %collective-permute-done.8.got = bf16[32,7168]{1,0:T(8,128)(2,1)S(1)} collective-permute-done((bf16[32,7168]{1,0:T(8,128)(2,1)S(1)}, bf16[32,7168]{1,0:T(8,128)(2,1)S(1)}, u32[]{:S(2)}, u32[]{:S(2)}) %collective-permute-start.8) | collective-permute-done | bytes 458784 | tf_op jit(solution)/shard_map/ppermute | solution.py:379
  34.6 0.1 sum.1
  34.7 2.8 %collective-permute-start.9 = (bf16[8,7168]{1,0:T(8,128)(2,1)S(1)}, bf16[8,7168]{1,0:T(8,128)(2,1)S(1)}, u32[]{:S(2)}, u32[]{:S(2)}) collective-permute-start(bf16[8,7168]{1,0:T(8,128)(2,1)S(1)} %get-tuple-element.76), channel_id=1, source_target_pairs={{0,8},{1,13},{2,10},{3,15},{4,12},{5,9},{6,14},{7,11},{8,0},{9,5},... | collective-permute-start | bytes 344072 | tf_op jit(solution)/shard_map/ppermute | solution.py:389
  37.6 0.9 %collective-permute-start.11 = (bf16[8,7168]{1,0:T(8,128)(2,1)S(1)}, bf16[8,7168]{1,0:T(8,128)(2,1)S(1)}, u32[]{:S(2)}, u32[]{:S(2)}) collective-permute-start(bf16[8,7168]{1,0:T(8,128)(2,1)S(1)} %get-tuple-element.84), channel_id=1, source_target_pairs={{0,10},{1,15},{2,8},{3,13},{4,14},{5,11},{6,12},{7,9},{8,2},{9,7},... | collective-permute-start | bytes 344072 | tf_op jit(solution)/shard_map/ppermute | solution.py:389
  38.4 0.4 collective-permute-start.12
  38.9 1.0 %collective-permute-start.10 = (bf16[8,3584]{1,0:T(8,128)(2,1)S(1)}, bf16[8,3584]{1,0:T(8,128)(2,1)S(1)}, u32[]{:S(2)}, u32[]{:S(2)}) collective-permute-start(bf16[8,3584]{1,0:T(8,128)(2,1)S(1)} %get-tuple-element.77), channel_id=1, source_target_pairs={{0,2},{1,3},{2,0},{3,1},{4,6},{5,7},{6,4},{7,5},{8,10},{9,11},{10,... | collective-permute-start | bytes 172040 | tf_op jit(solution)/shard_map/ppermute | solution.py:390
  39.9 4.9 %attention.1 = (bf16[4,8192]{1,0:T(4,128)(2,1)}, bf16[32,64]{1,0:T(8,128)(2,1)S(1)}) custom-call(s32[3,16]{1,0:T(4,128)S(1)} %bitcast.6, s32[3,16]{1,0:T(4,128)S(1)} %bitcast.7, s32[4]{0:T(128)} %refs_0_, bf16[4,8192]{1,0:T(4,128)(2,1)} %refs_1_.1, bf16[4,1024,256]{2,1,0:T(8,128)(2,1)} %refs_2_.1, bf16[4,1024,256]{2,1,0:T(8,128)(2,1)} %refs_3_.1), custom_call_target="tpu_custom_call" | custom-call | flops 134217728 | bytes 4194304 | tf_op jit(solution)/shard_map/attention/pallas_call | solution.py:395
  44.8 1.8 %collective-permute-done.9.refs_0_ = bf16[8,7168]{1,0:T(8,128)(2,1)S(1)} collective-permute-done((bf16[8,7168]{1,0:T(8,128)(2,1)S(1)}, bf16[8,7168]{1,0:T(8,128)(2,1)S(1)}, u32[]{:S(2)}, u32[]{:S(2)}) %collective-permute-start.9) | collective-permute-done | bytes 114720 | tf_op jit(solution)/shard_map/ppermute | solution.py:389
  46.6 0.0 collective-permute-start.13
  46.6 2.5 %collective-permute-done.11.refs_1_ = bf16[8,7168]{1,0:T(8,128)(2,1)S(1)} collective-permute-done((bf16[8,7168]{1,0:T(8,128)(2,1)S(1)}, bf16[8,7168]{1,0:T(8,128)(2,1)S(1)}, u32[]{:S(2)}, u32[]{:S(2)}) %collective-permute-start.11) | collective-permute-done | bytes 114720 | tf_op jit(solution)/shard_map/ppermute | solution.py:389
  49.1 0.5 collective-permute-start.15
  49.7 0.8 %collective-permute-done.14.refs_4_ = bf16[8,7168]{1,0:T(8,128)(2,1)S(1)} collective-permute-done((bf16[8,7168]{1,0:T(8,128)(2,1)S(1)}, bf16[8,7168]{1,0:T(8,128)(2,1)S(1)}, u32[]{:S(2)}, u32[]{:S(2)}) %collective-permute-start.14) | collective-permute-done | bytes 114720 | tf_op jit(solution)/shard_map/ppermute | solution.py:421
  50.5 0.2 collective-permute-done.15.refs_5_
  50.6 0.9 %combine.1 = bf16[16,3584]{1,0:T(8,128)(2,1)} custom-call(bf16[32,64]{1,0:T(8,128)(2,1)S(1)} %get-tuple-element.82.gates_ref, bf16[8,7168]{1,0:T(8,128)(2,1)S(1)} %collective-permute-done.9.refs_0_, bf16[8,7168]{1,0:T(8,128)(2,1)S(1)} %collective-permute-done.11.refs_1_, bf16[8,7168]{1,0:T(8,128)(2,1)S(1)} %collective-permute-done.12.refs_2_, ...), custom_call_target="tpu_custom_call" | custom-call | tf_op jit(solution)/shard_map/combine/pallas_call | solution.py:422
  (10 shorter events, 0.0 us)
Async XLA Ops:
  2.0 15.4 %collective-permute-start = (bf16[8,7168]{1,0:T(8,128)(2,1)S(1)}, bf16[8,7168]{1,0:T(8,128)(2,1)S(1)}, u32[]{:S(2)}, u32[]{:S(2)}) collective-permute-start(bf16[8,7168]{1,0:T(8,128)(2,1)S(1)} %get-tuple-element.45), channel_id=1, source_target_pairs={{0,8},{1,13},{2,10},{3,15},{4,12},{5,9},{6,14},{7,11},{8,0},{9,5},... | collective-permute-start | bytes 344072 | tf_op jit(solution)/shard_map/ppermute | solution.py:308
  6.1 11.6 %collective-permute-start.1 = (bf16[8,7168]{1,0:T(8,128)(2,1)S(1)}, bf16[8,7168]{1,0:T(8,128)(2,1)S(1)}, u32[]{:S(2)}, u32[]{:S(2)}) collective-permute-start(bf16[8,7168]{1,0:T(8,128)(2,1)S(1)} %get-tuple-element.46), channel_id=1, source_target_pairs={{0,10},{1,15},{2,8},{3,13},{4,14},{5,11},{6,12},{7,9},{8,2},{9,7},... | collective-permute-start | bytes 344072 | tf_op jit(solution)/shard_map/ppermute | solution.py:308
  7.3 10.3 %collective-permute-start.2 = (bf16[8,7168]{1,0:T(8,128)(2,1)S(1)}, bf16[8,7168]{1,0:T(8,128)(2,1)S(1)}, u32[]{:S(2)}, u32[]{:S(2)}) collective-permute-start(bf16[8,7168]{1,0:T(8,128)(2,1)S(1)} %get-tuple-element.47), channel_id=1, source_target_pairs={{0,4},{1,7},{2,6},{3,5},{4,0},{5,3},{6,2},{7,1},{8,12},{9,15},{10,... | collective-permute-start | bytes 344072 | tf_op jit(solution)/shard_map/ppermute | solution.py:308
  8.9 8.4 %collective-permute-start.3 = (bf16[8,3584]{1,0:T(8,128)(2,1)S(1)}, bf16[8,3584]{1,0:T(8,128)(2,1)S(1)}, u32[]{:S(2)}, u32[]{:S(2)}) collective-permute-start(bf16[8,3584]{1,0:T(8,128)(2,1)S(1)} %get-tuple-element.48), channel_id=1, source_target_pairs={{0,2},{1,3},{2,0},{3,1},{4,6},{5,7},{6,4},{7,5},{8,10},{9,11},{10,... | collective-permute-start | bytes 172040 | tf_op jit(solution)/shard_map/ppermute | solution.py:309
  17.7 1.9 %collective-permute-start.4 = (bf16[8,7168]{1,0:T(8,128)(2,1)S(1)}, bf16[8,7168]{1,0:T(8,128)(2,1)S(1)}, u32[]{:S(2)}, u32[]{:S(2)}) collective-permute-start(bf16[8,7168]{1,0:T(8,128)(2,1)S(1)} %collective-permute-done.refs_0_), channel_id=1, source_target_pairs={{0,1},{1,0},{2,3},{3,2},{4,5},{5,4},{6,7},{7,6},{8,9},{9,8},{10,11... | collective-permute-start | bytes 344072 | tf_op jit(solution)/shard_map/ppermute | solution.py:344
  17.7 1.9 %collective-permute-start.5 = (bf16[8,7168]{1,0:T(8,128)(2,1)S(1)}, bf16[8,7168]{1,0:T(8,128)(2,1)S(1)}, u32[]{:S(2)}, u32[]{:S(2)}) collective-permute-start(bf16[8,7168]{1,0:T(8,128)(2,1)S(1)} %collective-permute-done.1.refs_1_), channel_id=1, source_target_pairs={{0,1},{1,0},{2,3},{3,2},{4,5},{5,4},{6,7},{7,6},{8,9},{9,8},{10,11... | collective-permute-start | bytes 344072 | tf_op jit(solution)/shard_map/ppermute | solution.py:344
  18.2 1.4 %collective-permute-start.6 = (bf16[8,7168]{1,0:T(8,128)(2,1)S(1)}, bf16[8,7168]{1,0:T(8,128)(2,1)S(1)}, u32[]{:S(2)}, u32[]{:S(2)}) collective-permute-start(bf16[8,7168]{1,0:T(8,128)(2,1)S(1)} %collective-permute-done.2.refs_2_), channel_id=1, source_target_pairs={{0,1},{1,0},{2,3},{3,2},{4,5},{5,4},{6,7},{7,6},{8,9},{9,8},{10,11... | collective-permute-start | bytes 344072 | tf_op jit(solution)/shard_map/ppermute | solution.py:344
  18.2 1.4 %collective-permute-start.7 = (bf16[8,3584]{1,0:T(8,128)(2,1)S(1)}, bf16[8,3584]{1,0:T(8,128)(2,1)S(1)}, u32[]{:S(2)}, u32[]{:S(2)}) collective-permute-start(bf16[8,3584]{1,0:T(8,128)(2,1)S(1)} %collective-permute-done.3.refs_6_), channel_id=1, source_target_pairs={{0,1},{1,0},{2,3},{3,2},{4,5},{5,4},{6,7},{7,6},{8,9},{9,8},{10,11... | collective-permute-start | bytes 172040 | tf_op jit(solution)/shard_map/ppermute | solution.py:345
  32.7 7.2 %copy-start = (s32[16,3]{0,1:T(4,128)S(1)}, s32[16,3]{0,1:T(4,128)}, u32[]{:S(2)}) copy-start(s32[16,3]{0,1:T(4,128)} %param.15) | copy-start | bytes 580
  32.8 7.2 %copy-start.1 = (s32[16,3]{0,1:T(4,128)S(1)}, s32[16,3]{0,1:T(4,128)}, u32[]{:S(2)}) copy-start(s32[16,3]{0,1:T(4,128)} %param.16) | copy-start | bytes 580
  32.8 1.9 %collective-permute-start.8 = (bf16[32,7168]{1,0:T(8,128)(2,1)S(1)}, bf16[32,7168]{1,0:T(8,128)(2,1)S(1)}, u32[]{:S(2)}, u32[]{:S(2)}) collective-permute-start(bf16[32,7168]{1,0:T(8,128)(2,1)S(1)} %get-tuple-element.75), channel_id=1, source_target_pairs={{0,1},{1,0},{2,3},{3,2},{4,5},{5,4},{6,7},{7,6},{8,9},{9,8},{10,11... | collective-permute-start | bytes 1376264 | tf_op jit(solution)/shard_map/ppermute | solution.py:379
  34.7 11.9 %collective-permute-start.9 = (bf16[8,7168]{1,0:T(8,128)(2,1)S(1)}, bf16[8,7168]{1,0:T(8,128)(2,1)S(1)}, u32[]{:S(2)}, u32[]{:S(2)}) collective-permute-start(bf16[8,7168]{1,0:T(8,128)(2,1)S(1)} %get-tuple-element.76), channel_id=1, source_target_pairs={{0,8},{1,13},{2,10},{3,15},{4,12},{5,9},{6,14},{7,11},{8,0},{9,5},... | collective-permute-start | bytes 344072 | tf_op jit(solution)/shard_map/ppermute | solution.py:389
  37.6 11.6 %collective-permute-start.11 = (bf16[8,7168]{1,0:T(8,128)(2,1)S(1)}, bf16[8,7168]{1,0:T(8,128)(2,1)S(1)}, u32[]{:S(2)}, u32[]{:S(2)}) collective-permute-start(bf16[8,7168]{1,0:T(8,128)(2,1)S(1)} %get-tuple-element.84), channel_id=1, source_target_pairs={{0,10},{1,15},{2,8},{3,13},{4,14},{5,11},{6,12},{7,9},{8,2},{9,7},... | collective-permute-start | bytes 344072 | tf_op jit(solution)/shard_map/ppermute | solution.py:389
  38.4 10.7 %collective-permute-start.12 = (bf16[8,7168]{1,0:T(8,128)(2,1)S(1)}, bf16[8,7168]{1,0:T(8,128)(2,1)S(1)}, u32[]{:S(2)}, u32[]{:S(2)}) collective-permute-start(bf16[8,7168]{1,0:T(8,128)(2,1)S(1)} %get-tuple-element.85), channel_id=1, source_target_pairs={{0,4},{1,7},{2,6},{3,5},{4,0},{5,3},{6,2},{7,1},{8,12},{9,15},{10,... | collective-permute-start | bytes 344072 | tf_op jit(solution)/shard_map/ppermute | solution.py:389
  38.9 5.9 %collective-permute-start.10 = (bf16[8,3584]{1,0:T(8,128)(2,1)S(1)}, bf16[8,3584]{1,0:T(8,128)(2,1)S(1)}, u32[]{:S(2)}, u32[]{:S(2)}) collective-permute-start(bf16[8,3584]{1,0:T(8,128)(2,1)S(1)} %get-tuple-element.77), channel_id=1, source_target_pairs={{0,2},{1,3},{2,0},{3,1},{4,6},{5,7},{6,4},{7,5},{8,10},{9,11},{10,... | collective-permute-start | bytes 172040 | tf_op jit(solution)/shard_map/ppermute | solution.py:390
  46.6 3.1 %collective-permute-start.13 = (bf16[8,7168]{1,0:T(8,128)(2,1)S(1)}, bf16[8,7168]{1,0:T(8,128)(2,1)S(1)}, u32[]{:S(2)}, u32[]{:S(2)}) collective-permute-start(bf16[8,7168]{1,0:T(8,128)(2,1)S(1)} %collective-permute-done.9.refs_0_), channel_id=1, source_target_pairs={{0,1},{1,0},{2,3},{3,2},{4,5},{5,4},{6,7},{7,6},{8,9},{9,8},{10,11... | collective-permute-start | bytes 344072 | tf_op jit(solution)/shard_map/ppermute | solution.py:421
  49.1 1.3 %collective-permute-start.14 = (bf16[8,7168]{1,0:T(8,128)(2,1)S(1)}, bf16[8,7168]{1,0:T(8,128)(2,1)S(1)}, u32[]{:S(2)}, u32[]{:S(2)}) collective-permute-start(bf16[8,7168]{1,0:T(8,128)(2,1)S(1)} %collective-permute-done.11.refs_1_), channel_id=1, source_target_pairs={{0,1},{1,0},{2,3},{3,2},{4,5},{5,4},{6,7},{7,6},{8,9},{9,8},{10,11... | collective-permute-start | bytes 344072 | tf_op jit(solution)/shard_map/ppermute | solution.py:421
  49.1 1.5 %collective-permute-start.15 = (bf16[8,7168]{1,0:T(8,128)(2,1)S(1)}, bf16[8,7168]{1,0:T(8,128)(2,1)S(1)}, u32[]{:S(2)}, u32[]{:S(2)}) collective-permute-start(bf16[8,7168]{1,0:T(8,128)(2,1)S(1)} %collective-permute-done.12.refs_2_), channel_id=1, source_target_pairs={{0,1},{1,0},{2,3},{3,2},{4,5},{5,4},{6,7},{7,6},{8,9},{9,8},{10,11... | collective-permute-start | bytes 344072 | tf_op jit(solution)/shard_map/ppermute | solution.py:421
